TPU v7x, 512 devices: a whole 4x8x8 slice. The times are simulated.
512 devices in a mesh: patch: 128 (over y_hi, x, z, core), lev: 4 (over y_lo).
Axes of the slice: x: 4, y: 8 (y_hi: 2, y_lo: 4; y = y_hi * 4 + y_lo), z: 8, core: 2. Of those that a mesh axis runs over, the one named last changes fastest.
Arguments:
- prior_mean: float32 [4, 65536], P('lev', 'patch'), may hold values from -4 to 4
- prior_pert: float32 [80, 4, 65536], P(None, 'lev', 'patch'), may hold values from -4 to 4
- obs_value: float32 [8, 3072], replicated, may hold values from -12 to 12
- obs_var: float32 [8, 3072], replicated, may hold values from 6 to 24
- obs_cell: int32 [8, 3072], replicated, may hold values from 0 to 511
- obs_level: int32 [8, 3072], replicated, may hold values from 0 to 3
- obs_count: int32 [8, 128], replicated, may hold values from 1 to 24, 1024 in all within a row
- batch_order: int32 [8], replicated, may hold values from 0 to 7, each once
- horiz_weight: float32 [16], replicated, may hold values from 0.4 to 1
- vert_weight: float32 [4], replicated, may hold values from 0.4 to 1
Outputs:
- post_mean: float32 [4, 65536], P('lev', 'patch')
- post_pert: float32 [80, 4, 65536], P(None, 'lev', 'patch')
Inputs may be any that keep to these rules, and one draw needn't show every extreme that they name: `obs_count`: each batch's counts sum to 1024; in every batch some patch has exactly 24 live observations. `batch_order`: each batch number appears once.
All inputs are finite; a program needn't handle non-finite values.
Results may differ from a plain program's by a relative error of at most 0.003.
Values may be sent and summed in bfloat16 or wider, within the bound.
No kernel may reach another device: no remote copies, remote signals or barrier semaphores. Data moves between devices by JAX's collectives and lax.ppermute only.
A program may use at most 64 MiB of HBM per device.

v0:
```python
import jax
import jax.numpy as jnp
from jax import lax
from jax.sharding import PartitionSpec as P

TX = 16
TY = 32
LEV_DEV = 1
NBATCH = 6
PROWS = 8
NBIN = 16
CAP = 24


def lookup(bins, table):
    hits = bins[..., None] == jnp.arange(table.shape[0], dtype=jnp.int32)
    return jnp.sum(jnp.where(hits, table, jnp.zeros_like(table)), axis=-1)


def block_terms(piece, obs_x, obs_y, obs_lev, obs_err, grid, tables, pert_bf):
    own_x, own_y, own_lev, span_x, width_bin = grid
    horiz_weight, vert_weight = tables
    members = pert_bf.shape[0]
    values = piece.astype(jnp.float32)
    spread = jnp.sum(values[:members] * values[:members], axis=0) / (members - 1.0) + obs_err
    shrink = 1.0 / (1.0 + jnp.sqrt(obs_err / spread))
    nbins = horiz_weight.shape[0]
    dist_x = jnp.abs(obs_x[:, None] - own_x[None, :])
    dist_x = jnp.minimum(dist_x, span_x - dist_x)
    weight_x = lookup(jnp.minimum(dist_x // width_bin, nbins - 1), horiz_weight)
    dist_y = jnp.abs(obs_y[:, None] - own_y[None, :])
    weight_y = lookup(jnp.minimum(dist_y // width_bin, nbins - 1), horiz_weight)
    weight_z = lookup(jnp.abs(obs_lev[:, None] - own_lev[None, :]), vert_weight)
    rows = piece.shape[1]
    taper = (
        weight_z[:, :, None, None] * weight_x[:, None, :, None] * weight_y[:, None, None, :]
    ).reshape(rows, -1)
    covar = lax.dot_general(
        piece[:members], pert_bf, (((0,), (0,)), ((), ())), preferred_element_type=jnp.float32
    )
    scaled = (taper * covar * (1.0 / ((members - 1.0) * spread))[:, None]).astype(jnp.bfloat16)
    coeffs = jnp.concatenate([values[:members] * shrink[None, :], values[members:]], axis=0).astype(
        jnp.bfloat16
    )
    return jnp.dot(coeffs, scaled, preferred_element_type=jnp.float32)


def all_terms(piece, meta, grid, tables, pert_bf):
    obs_x, obs_y, obs_lev, obs_err = meta
    rows = piece.shape[1]
    size = 512
    count = -(-rows // size)
    blocks = (
        piece.reshape(piece.shape[0], count, size).transpose(1, 0, 2),
        obs_x.reshape(count, size),
        obs_y.reshape(count, size),
        obs_lev.reshape(count, size),
        obs_err.reshape(count, size),
    )

    def accumulate(total, item):
        return (
            total + block_terms(item[0], item[1], item[2], item[3], item[4], grid, tables, pert_bf),
            None,
        )

    start = jnp.zeros((piece.shape[0], pert_bf.shape[1]), jnp.float32)
    total, unused = lax.scan(accumulate, start, blocks)
    return total


def shards(
    prior_mean,
    prior_pert,
    obs_value,
    obs_var,
    obs_cell,
    obs_level,
    obs_count,
    batch_order,
    horiz_weight,
    vert_weight,
):
    members = prior_pert.shape[0]
    npatch = lax.axis_size("patch")
    patch_idx = lax.axis_index("patch")
    lev_idx = lax.axis_index("lev")
    cols = TX * TY
    cells = LEV_DEV * cols
    span_x = TX * (npatch // PROWS)
    span_y = TY * PROWS
    width_bin = (max(span_x // 2, span_y) + NBIN - 1) // NBIN
    own_x = patch_idx // PROWS * TX + jnp.arange(TX, dtype=jnp.int32)
    own_y = patch_idx % PROWS * TY + jnp.arange(TY, dtype=jnp.int32)
    own_lev = lev_idx * LEV_DEV + jnp.arange(LEV_DEV, dtype=jnp.int32)
    grid = (own_x, own_y, own_lev, span_x, width_bin)
    tables = (horiz_weight, vert_weight)
    patches = jnp.arange(npatch, dtype=jnp.int32)
    tile_x = patches // PROWS * TX
    tile_y = patches % PROWS * TY
    mean_loc = prior_mean.reshape(cells)
    pert_loc = prior_pert.reshape(members, cells)
    for step in range(NBATCH):
        pick = batch_order[step]
        cell_b = lax.dynamic_index_in_dim(obs_cell, pick, 0, keepdims=False)
        lev_b = lax.dynamic_index_in_dim(obs_level, pick, 0, keepdims=False)
        value_b = lax.dynamic_index_in_dim(obs_value, pick, 0, keepdims=False)
        err_b = lax.dynamic_index_in_dim(obs_var, pick, 0, keepdims=False)
        count_b = lax.dynamic_index_in_dim(obs_count, pick, 0, keepdims=False)
        live_all = (jnp.arange(CAP, dtype=jnp.int32)[None, :] < count_b[:, None]).reshape(-1)
        cell_grid = cell_b.reshape(npatch, CAP)
        obs_x = (tile_x[:, None] + cell_grid // TY).reshape(-1)
        obs_y = (tile_y[:, None] + cell_grid % TY).reshape(-1)
        metas = (obs_x, obs_y, lev_b, err_b)
        own_cell = lax.dynamic_slice_in_dim(cell_b, patch_idx * CAP, CAP)
        own_level = lax.dynamic_slice_in_dim(lev_b, patch_idx * CAP, CAP)
        own_value = lax.dynamic_slice_in_dim(value_b, patch_idx * CAP, CAP)
        own_live = lax.dynamic_slice_in_dim(live_all, patch_idx * CAP, CAP)
        keep = own_live & (own_level // LEV_DEV == lev_idx)
        where_at = jnp.clip((own_level - lev_idx * LEV_DEV) * cols + own_cell, 0, cells - 1)
        first = jnp.take(pert_loc, where_at, axis=1)
        head = jnp.take(mean_loc, where_at)
        innov = jnp.where(keep, own_value - head, jnp.zeros_like(head))
        first = jnp.where(keep[None, :], first, jnp.zeros_like(first))
        stacked = jnp.concatenate([first, innov[None, :]], axis=0)
        pert_bf = pert_loc.astype(jnp.bfloat16)
        prior = lax.psum(stacked, "lev").astype(jnp.bfloat16)
        meta = tuple((item for item in metas))
        collected = all_terms(
            lax.all_gather(prior, "patch", axis=1, tiled=True), meta, grid, tables, pert_bf
        )
        pert_loc = pert_loc - collected[:members]
        mean_loc = mean_loc + collected[members]
    return (mean_loc.reshape(prior_mean.shape), pert_loc.reshape(prior_pert.shape))


def solution(mesh):
    return jax.shard_map(
        shards,
        mesh=mesh,
        in_specs=(
            P("lev", "patch"),
            P(None, "lev", "patch"),
            P(),
            P(),
            P(),
            P(),
            P(),
            P(),
            P(),
            P(),
        ),
        out_specs=(P("lev", "patch"), P(None, "lev", "patch")),
        check_vma=False,
    )
```

profile of v0, /device:TPU:1, one launch (start us, length us, event | category | flops | bytes accessed | tf_op | source)
XLA Modules:
  0.0 1604.4 jit_solution(8242262200164268232)
XLA Ops:
  0.6 1.6 fusion.200
  13.6 1.5 fusion.182
  15.4 1.6 compare_and_fusion
  20.2 16.0 psum.42
  36.2 233.4 %all_gather.18 = bf16[81,3072]{0,1:T(8,128)(2,1)S(1)} all-gather(bf16[81,24]{0,1:T(8,128)(2,1)S(1)} %psum.42), channel_id=1, replica_groups=mesh['patch'=128,'lev'=4] {'patch'}, dimensions={1}, use_global_device_ids=true | all-gather | bytes 501552 | tf_op jit(solution)/shard_map/all_gather | solution.py:130
  274.5 12.1 while.84
  289.2 12.1 psum.43
  301.3 218.9 %all_gather.19 = bf16[81,3072]{0,1:T(8,128)(2,1)S(1)} all-gather(bf16[81,24]{0,1:T(8,128)(2,1)S(1)} %psum.43), channel_id=1, replica_groups=mesh['patch'=128,'lev'=4] {'patch'}, dimensions={1}, use_global_device_ids=true | all-gather | bytes 501552 | tf_op jit(solution)/shard_map/all_gather | solution.py:130
  520.7 12.1 while.85
  536.9 12.4 psum.44
  549.3 221.4 %all_gather.20 = bf16[81,3072]{0,1:T(8,128)(2,1)S(1)} all-gather(bf16[81,24]{0,1:T(8,128)(2,1)S(1)} %psum.44), channel_id=1, replica_groups=mesh['patch'=128,'lev'=4] {'patch'}, dimensions={1}, use_global_device_ids=true | all-gather | bytes 501552 | tf_op jit(solution)/shard_map/all_gather | solution.py:130
  772.5 21.9 %while.86 = (s32[]{:T(128)}, f32[81,512]{1,0:T(8,128)S(1)}, bf16[6,81,512]{2,1,0:T(8,128)(2,1)S(1)}, f32[6,512]{1,0:T(8,128)S(1)}, s32[6,512]{1,0:T(8,128)}, /*i...) while((s32[]{:T(128)}, f32[81,512]{1,0:T(8,128)S(1)}, ...), condition=%wide.region_20.23_spmd.clone, body=%wide.region_15.22_spmd.clone.sunk | while | flops 87586352 | bytes 5640991 | solution.py:68
  798.3 12.1 psum.45
  810.3 218.8 %all_gather.21 = bf16[81,3072]{0,1:T(8,128)(2,1)S(1)} all-gather(bf16[81,24]{0,1:T(8,128)(2,1)S(1)} %psum.45), channel_id=1, replica_groups=mesh['patch'=128,'lev'=4] {'patch'}, dimensions={1}, use_global_device_ids=true | all-gather | bytes 501552 | tf_op jit(solution)/shard_map/all_gather | solution.py:130
  1030.9 20.7 %while.87 = (s32[]{:T(128)}, f32[81,512]{1,0:T(8,128)S(1)}, bf16[6,81,512]{2,1,0:T(8,128)(2,1)S(1)}, f32[6,512]{1,0:T(8,128)S(1)}, s32[6,512]{1,0:T(8,128)S(1)},...) while((s32[]{:T(128)}, f32[81,512]{1,0:T(8,128)S(1)}, ...), condition=%wide.region_27.30_spmd.clone, body=%wide.region_22.29_spmd.clone.sunk | while | flops 87586352 | bytes 5542631 | solution.py:68
  1057.7 12.5 psum.46
  1070.2 221.1 %all_gather.22 = bf16[81,3072]{0,1:T(8,128)(2,1)S(1)} all-gather(bf16[81,24]{0,1:T(8,128)(2,1)S(1)} %psum.46), channel_id=1, replica_groups=mesh['patch'=128,'lev'=4] {'patch'}, dimensions={1}, use_global_device_ids=true | all-gather | bytes 501552 | tf_op jit(solution)/shard_map/all_gather | solution.py:130
  1293.7 30.0 %while.88 = (s32[]{:T(128)}, f32[81,512]{1,0:T(8,128)S(1)}, bf16[6,81,512]{2,1,0:T(8,128)(2,1)S(1)}, f32[6,512]{1,0:T(8,128)}, s32[6,512]{1,0:T(8,128)}, /*index...) while((s32[]{:T(128)}, f32[81,512]{1,0:T(8,128)S(1)}, ...), condition=%wide.region_34.37_spmd.clone, body=%wide.region_29.36_spmd.clone.sunk | while | flops 87586352 | bytes 5870339 | solution.py:68
  1328.4 12.1 psum.47
  1340.5 219.1 %all_gather.23 = bf16[81,3072]{0,1:T(8,128)(2,1)S(1)} all-gather(bf16[81,24]{0,1:T(8,128)(2,1)S(1)} %psum.47), channel_id=1, replica_groups=mesh['patch'=128,'lev'=4] {'patch'}, dimensions={1}, use_global_device_ids=true | all-gather | bytes 501552 | tf_op jit(solution)/shard_map/all_gather | solution.py:130
  1562.1 40.7 %while.89 = (s32[]{:T(128)}, f32[81,512]{1,0:T(8,128)S(1)}, bf16[6,81,512]{2,1,0:T(8,128)(2,1)}, f32[6,512]{1,0:T(8,128)S(1)}, s32[6,512]{1,0:T(8,128)}, /*index...) while((s32[]{:T(128)}, f32[81,512]{1,0:T(8,128)S(1)}, ...), condition=%wide.region_41.44_spmd.clone, body=%wide.region_36.43_spmd.clone.sunk | while | flops 87586352 | bytes 5527779 | solution.py:68
  1567.5 1.4 fusion.290
  1587.8 1.4 fusion.290
  1594.6 1.4 fusion.290
  (900 shorter events, 169.0 us)
Async XLA Ops:
  0.6 14.8 copy-start.13
  17.7 1.5 copy-start.10
  269.6 0.9 copy-start.14
  272.0 0.9 copy-start.15
  286.7 1.3 copy-start.6
  532.8 1.0 copy-start.7
  772.5 1.6 copy-start.24
  776.1 1.6 copy-start.24
  779.8 1.6 copy-start.24
  783.4 1.6 copy-start.24
  787.0 1.6 copy-start.24
  790.7 1.6 copy-start.24
  794.5 1.3 copy-start.4
  795.8 0.7 copy-start.12
  1051.6 1.0 copy-start.5
  1052.6 1.3 copy-start.2
  1291.6 0.7 copy-start.17
  1297.2 0.9 copy-start.1
  1302.3 0.9 copy-start.1
  1307.3 0.9 copy-start.1
  1312.3 0.9 copy-start.1
  1317.3 0.9 copy-start.1
  1322.3 0.9 copy-start.1
  1323.7 1.0 copy-start.3
  (25 other events, 17.2 us)
where the time goes:
time: 1610 us; the launch traced here: 1600 us
  blocking collectives  1410 us (88%)
  other arithmetic  80 us (5%)
  local copies, waits for them, and re-layouts  74.4 us (5%)
  matrix products  23.5 us (1%)
    all_gather x6, blocking collectives, shards(): lax.all_gather(prior, 'patch', axis=1, tiled=True)  1330 us
    psum x6, blocking collectives, shards(): prior = lax.psum(stacked, 'lev').astype(jnp.bfloat16)  77.1 us

commit v1 on v0

v1 whole, which is shorter than its diff:
```python
import functools

import jax
import jax.numpy as jnp
from jax import lax
from jax.experimental import pallas as pl
from jax.experimental.pallas import tpu as pltpu
from jax.sharding import PartitionSpec as P

TX = 16
TY = 32
NBATCH = 6
PROWS = 8
NBIN = 16
CAP = 24
NOBS = 1024
CELLS = TX * TY
ROWS = 88
WIDE = 128
TILE = 512
LIVE_COLS = NBATCH * NOBS
COLS = LIVE_COLS + CELLS
UNIT = 1.0 / 16.0


def select_kernel(order_ref, where_ref, count_ref, cell_ref, lev_ref, value_ref, var_ref, pert_ref, mean_ref, out_ref):
    patch = where_ref[0]
    level = where_ref[1]

    def ordered(ref):
        rows = [ref[pl.ds(order_ref[k], 1), :] for k in range(NBATCH)]
        return jnp.concatenate(rows + [rows[-1], rows[-1]], axis=0)

    count = ordered(count_ref)
    lane = lax.broadcasted_iota(jnp.int32, count.shape, 1)
    zero = jnp.zeros_like(count)
    first = jnp.sum(jnp.where(lane < patch, count, zero), axis=1, keepdims=True)
    held = jnp.sum(jnp.where(lane == patch, count, zero), axis=1, keepdims=True)
    cell, lev, value, var = ordered(cell_ref), ordered(lev_ref), ordered(value_ref), ordered(var_ref)
    slot = lax.broadcasted_iota(jnp.int32, (8, NOBS), 1) - first
    cell_at = jnp.zeros((8, NOBS), jnp.int32)
    lev_at = jnp.full((8, NOBS), -1, jnp.int32)
    value_at = jnp.zeros((8, NOBS), jnp.float32)
    var_at = jnp.zeros((8, NOBS), jnp.float32)
    for s in range(CAP):
        here = slot == s
        cell_at = jnp.where(here, cell[:, s : s + 1], cell_at)
        lev_at = jnp.where(here, lev[:, s : s + 1], lev_at)
        value_at = jnp.where(here, value[:, s : s + 1], value_at)
        var_at = jnp.where(here, var[:, s : s + 1], var_at)
    own = (slot >= 0) & (slot < held) & (lev_at == level)
    none = jnp.zeros((8, NOBS), jnp.float32)
    pick = jnp.where(own, cell_at, -1)
    var_at = jnp.where(own, var_at, none)
    obs_x = jnp.where(own, (patch // PROWS * TX + cell_at // TY).astype(jnp.float32) * UNIT, none)
    obs_y = jnp.where(own, (patch % PROWS * TY + cell_at % TY).astype(jnp.float32) * UNIT, none)
    obs_z = jnp.where(own, lev_at.astype(jnp.float32) * NBIN, none)
    owned = jnp.where(own, none + 1.0, none)

    state = jnp.concatenate([pert_ref[...], mean_ref[...], jnp.zeros((ROWS - 81, CELLS), jnp.float32)], axis=0)
    high = state.astype(jnp.bfloat16)
    rest = state - high.astype(jnp.float32)
    mid = rest.astype(jnp.bfloat16)
    low = (rest - mid.astype(jnp.float32)).astype(jnp.bfloat16)
    spot = lax.broadcasted_iota(jnp.int32, (CELLS, NOBS), 0)
    for k in range(NBATCH):
        hot = (spot == pick[k : k + 1, :]).astype(jnp.float32).astype(jnp.bfloat16)
        taken = (
            jnp.dot(high, hot, preferred_element_type=jnp.float32)
            + jnp.dot(mid, hot, preferred_element_type=jnp.float32)
            + jnp.dot(low, hot, preferred_element_type=jnp.float32)
        )
        innov = (value_at[k : k + 1] - taken[80:81]) * owned[k : k + 1]
        tail = [innov, var_at[k : k + 1], obs_x[k : k + 1], obs_y[k : k + 1], obs_z[k : k + 1]]
        block = jnp.concatenate([taken[:80]] + tail + [jnp.zeros((3, NOBS), jnp.float32)], axis=0)
        out_ref[:, k * NOBS : (k + 1) * NOBS] = block


def filter_kernel(where_ref, obs_ref, pert_ref, mean_ref, near_ref, far_ref, post_pert_ref, post_mean_ref, state, cov, gain):
    patch = where_ref[0]
    level = where_ref[1]
    for k in range(NBATCH):
        block = jnp.concatenate(
            [obs_ref[:, k * NOBS : (k + 1) * NOBS], jnp.zeros((WIDE - ROWS, NOBS), jnp.float32)], axis=0
        )
        state[k * NOBS : (k + 1) * NOBS, :] = block.T
    spot = lax.broadcasted_iota(jnp.int32, (1, CELLS), 1)
    own_x = (patch // PROWS * TX + spot // TY).astype(jnp.float32) * UNIT
    own_y = (patch % PROWS * TY + spot % TY).astype(jnp.float32) * UNIT
    own_z = jnp.zeros((1, CELLS), jnp.float32) + (level * NBIN).astype(jnp.float32)
    block = jnp.concatenate(
        [
            pert_ref[...],
            -mean_ref[...],
            jnp.zeros((1, CELLS), jnp.float32),
            own_x,
            own_y,
            own_z,
            jnp.zeros((WIDE - 85, CELLS), jnp.float32),
        ],
        axis=0,
    )
    state[LIVE_COLS:COLS, :] = block.T
    near = jnp.broadcast_to(near_ref[...], (TILE, WIDE))
    far = jnp.broadcast_to(far_ref[...], (TILE, WIDE))
    span = float(PROWS * TY) * UNIT

    def batch(k, unused):
        start = pl.multiple_of(k * NOBS, NOBS)
        block = state[pl.ds(start, NOBS), :].T
        prior = block.astype(jnp.bfloat16).astype(jnp.float32)
        row = lax.broadcasted_iota(jnp.int32, (WIDE, NOBS), 0)
        members = jnp.where(row < 80, prior, jnp.zeros_like(prior))
        obs_var = block[81:82]
        spread = jnp.sum(members * members, axis=0, keepdims=True) / 79.0 + obs_var
        shrink = 1.0 / (1.0 + jnp.sqrt(obs_var / spread))
        scale = 1.0 / (79.0 * spread)
        coeffs = jnp.where(row == 80, prior, members * shrink).T.astype(jnp.bfloat16)
        members = members.astype(jnp.bfloat16)
        obs_x, obs_y, obs_z = block[82:83], block[83:84], block[84:85]

        def tile(t, unused):
            at = pl.multiple_of(t * TILE, TILE)
            cells = state[pl.ds(at, TILE), :]
            cov[...] = jnp.dot(cells.astype(jnp.bfloat16), members, preferred_element_type=jnp.float32)
            cell_x, cell_y, cell_z = cells[:, 82:83], cells[:, 83:84], cells[:, 84:85]
            for j in range(NOBS // WIDE):
                part = slice(j * WIDE, (j + 1) * WIDE)
                dist_x = jnp.abs(obs_x[:, part] - cell_x)
                dist_x = jnp.minimum(dist_x, span - dist_x) + jnp.abs(obs_z[:, part] - cell_z)
                dist_y = jnp.abs(obs_y[:, part] - cell_y)
                taper = jnp.take_along_axis(near, dist_x.astype(jnp.int32), axis=1) * jnp.take_along_axis(
                    far, dist_y.astype(jnp.int32), axis=1
                )
                gain[:, part] = (taper * cov[:, part] * scale[:, part]).astype(jnp.bfloat16)
            change = jnp.dot(gain[...], coeffs, preferred_element_type=jnp.float32)
            state[pl.ds(at, TILE), :] = cells - change
            return unused

        return lax.fori_loop((k + 1) * (NOBS // TILE), COLS // TILE, tile, unused)

    lax.fori_loop(0, NBATCH, batch, 0)
    block = state[LIVE_COLS:COLS, :].T
    post_pert_ref[...] = block[:80]
    post_mean_ref[...] = -block[80:81]


VMEM = pltpu.VMEM
SMEM = pltpu.SMEM


def select_call(order, where, count, cell, lev, value, var, pert, mean):
    return pl.pallas_call(
        select_kernel,
        out_shape=jax.ShapeDtypeStruct((ROWS, LIVE_COLS), jnp.float32),
        in_specs=[pl.BlockSpec(memory_space=SMEM)] * 2 + [pl.BlockSpec(memory_space=VMEM)] * 7,
        out_specs=pl.BlockSpec(memory_space=VMEM),
        compiler_params=pltpu.CompilerParams(vmem_limit_bytes=48 << 20),
    )(order, where, count, cell, lev, value, var, pert, mean)


def filter_call(where, obs, pert, mean, near, far):
    return pl.pallas_call(
        filter_kernel,
        out_shape=(
            jax.ShapeDtypeStruct((80, CELLS), jnp.float32),
            jax.ShapeDtypeStruct((1, CELLS), jnp.float32),
        ),
        in_specs=[pl.BlockSpec(memory_space=SMEM)] + [pl.BlockSpec(memory_space=VMEM)] * 5,
        out_specs=(pl.BlockSpec(memory_space=VMEM),) * 2,
        scratch_shapes=[
            VMEM((COLS, WIDE), jnp.float32),
            VMEM((TILE, NOBS), jnp.float32),
            VMEM((TILE, NOBS), jnp.bfloat16),
        ],
        compiler_params=pltpu.CompilerParams(vmem_limit_bytes=48 << 20),
    )(where, obs, pert, mean, near, far)


def shards(
    prior_mean,
    prior_pert,
    obs_value,
    obs_var,
    obs_cell,
    obs_level,
    obs_count,
    batch_order,
    horiz_weight,
    vert_weight,
):
    patch = lax.axis_index("patch")
    where = jnp.stack([patch, lax.axis_index("lev")]).astype(jnp.int32)
    pert = prior_pert.reshape(80, CELLS)
    mean = prior_mean.reshape(1, CELLS)
    own = [lax.dynamic_slice_in_dim(item, patch * CAP, CAP, 1) for item in (obs_cell, obs_level, obs_value, obs_var)]
    obs = select_call(batch_order, where, obs_count, *own, pert, mean)
    obs = lax.psum(obs, ("patch", "lev"))
    near = jnp.pad((vert_weight[:, None] * horiz_weight[None, :]).reshape(1, -1), ((0, 0), (0, 64)))
    far = jnp.pad(horiz_weight[None, :], ((0, 0), (0, 112)))
    post_pert, post_mean = filter_call(where, obs, pert, mean, near, far)
    return post_mean.reshape(prior_mean.shape), post_pert.reshape(prior_pert.shape)


def solution(mesh):
    return jax.shard_map(
        shards,
        mesh=mesh,
        in_specs=(
            P("lev", "patch"),
            P(None, "lev", "patch"),
            P(),
            P(),
            P(),
            P(),
            P(),
            P(),
            P(),
            P(),
        ),
        out_specs=(P("lev", "patch"), P(None, "lev", "patch")),
        check_vma=False,
    )
```

time: 1610 us -> 447 us (0.28)
  blocking collectives: 1410 us -> 0 us
  waiting for transfers between devices: 0 us -> 285 us
  Pallas kernels: 0 us -> 140 us
  other arithmetic: 80 us -> 0.15 us
  local copies, waits for them, and re-layouts: 74.4 us -> 7.09 us
  matrix products: 23.5 us -> 0 us
    all_gather x6 -> x0, blocking collectives: 1330 us -> none  [shards(): lax.all_gather(prior, 'patch', axis=1, tiled=True)]
    psum x0 -> x1, waiting for transfers between devices: none -> 285 us  [shards(): obs = lax.psum(obs, ('patch', 'lev'))]
    pallas_call x0 -> x2, Pallas kernels: none -> 140 us  [the longest x1 134 us: filter_call(): pl.pallas_call(filter_kernel, out_shape=(jax.ShapeDtypeStruct((80, CELLS)...]
    psum x6 -> x0, blocking collectives: 77.1 us -> none  [shards(): prior = lax.psum(stacked, 'lev').astype(jnp.bfloat16)]
    reduce_sum x144 -> x0, other arithmetic: 27 us -> none  [the longest x108 20.1 us: lookup(): return jnp.sum(jnp.where(hits, table, jnp.zeros_like(table)), axis=-1)]
    dot_general x36 -> x0, matrix products: 23.5 us -> none  [block_terms(): return jnp.dot(coeffs, scaled, preferred_element_type=jnp.float32)]
    abs x36 -> x0, other arithmetic: 17.9 us -> none  [block_terms(): weight_z = lookup(jnp.abs(obs_lev[:, None] - own_lev[None, :]), vert_weight)]
    dynamic_slice x38 -> x2, local copies, waits for them, and re-layouts: 19.2 us -> 1.58 us  [shards(): lax.dynamic_slice_in_dim(item, patch * CAP, CAP, 1)]
  transfers between devices with their start and end apart: 0 -> 1, of which waited for: 0 -> 1; matrix products, arithmetic and copies ran while one was open for 0% -> 0% of each run, Pallas kernels for 0% -> 0%
where the time goes in v1:
time: 447 us; the launch traced here: 446 us
  waiting for transfers between devices  285 us (64%)
  Pallas kernels  140 us (31%)
  between operations  14.1 us (3%)
  local copies, waits for them, and re-layouts  7.09 us (2%)
    psum x1, waiting for transfers between devices, shards(): obs = lax.psum(obs, ('patch', 'lev'))  285 us
    pallas_call x1, Pallas kernels, filter_call(): pl.pallas_call(filter_kernel, out_shape=(jax.ShapeDtypeStruct((80, CELLS)...  134 us
  transfers between devices with their start and end apart: 1, of which 1 were waited for; matrix products, arithmetic and copies ran while one was open for 0% of the time, Pallas kernels for 0%

profile of v1, /device:TPU:1, one launch (start us, length us, event | category | flops | bytes accessed | tf_op | source)
XLA Modules:
  0.0 446.0 jit_solution(5164746990271646257)
XLA Ops:
  7.2 0.0 all-reduce.4.cloned.1.call-start
  7.2 0.9 copy.15
  8.1 0.8 constant_dynamic-slice_fusion.2
  8.9 0.8 constant_dynamic-slice_fusion
  9.7 0.1 pad_add_fusion.where_ref
  9.8 0.7 copy-done.1
  10.5 0.0 copy-start.3
  10.5 0.7 copy-done.3
  11.2 0.0 copy-start.4
  11.2 0.7 copy-done.4
  11.8 0.0 copy-start.5
  11.8 0.0 copy-start.6
  11.8 0.0 copy-start.2
  11.8 5.9 %shard_map.113 = f32[88,6144]{1,0:T(8,128)} custom-call(s32[8]{0:T(128)S(1)} %copy-done.4, s32[2]{0:T(128)S(1)} %pad_add_fusion.where_ref, s32[8,128]{1,0:T(8,128)S(1)} %copy-done.3, s32[8,24]{1,0:T(8,128)S(1)} %get-tuple-element.11.cell_ref, s32[8,24]{1,0:T(8,128)S(1)} %get-tuple-element.10.lev_ref, f32[8,24]{1,0:T(8,128)S(1)} %get-tuple-element.9.value_ref, ...), custom_call_target="tpu_custom_call" | custom-call | tf_op jit(solution)/shard_map/pallas_call | solution.py:153
  17.7 0.0 all-reduce.4.cloned.1.call-update
  17.7 0.0 copy-done.5
  17.7 0.0 copy-done.6
  17.7 0.1 broadcast_multiply_fusion
  17.8 0.1 mul.33
  17.9 285.1 %all-reduce.4.cloned.1.call-done.obs_ref = f32[88,6144]{1,0:T(8,128)} async-done(((f32[88,6144]{1,0:T(8,128)}), f32[88,6144]{1,0:T(8,128)}) %all-reduce.4.cloned.1.call-update) | async-done | bytes 2162704 | tf_op jit(solution)/shard_map/psum | solution.py:198
  303.0 0.0 copy-done.2
  303.0 1.6 copy-done
  304.6 133.8 %shard_map.114 = (f32[80,512]{1,0:T(8,128)S(1)}, f32[1,512]{1,0:T(1,128)}) custom-call(s32[2]{0:T(128)S(1)} %pad_add_fusion.where_ref, f32[88,6144]{1,0:T(8,128)S(1)} %copy-done, f32[80,512]{1,0:T(8,128)S(1)} %bitcast.8, f32[1,512]{1,0:T(1,128)S(1)} %copy-done.2, f32[1,128]{1,0:T(1,128)S(1)} %pad.8.near_ref, f32[1,128]{1,0:T(1,128)S(1)} %pad.9.far_ref), custom_call_target="tpu_custom_call" | custom-call | tf_op jit(solution)/shard_map/pallas_call | solution.py:163
  438.4 0.8 copy.12
  (4 shorter events, 0.0 us)
Async XLA Ops:
  7.2 295.8 %all-reduce.4.cloned.1.call-start = ((), (), s32[]{:S(2)}) async-start(), calls=%async_computation | async-start | bytes 4325376 | tf_op jit(solution)/shard_map/psum | solution.py:198
  9.8 0.7 copy-start.1
  10.5 0.7 copy-start.3
  11.2 0.7 copy-start.4
  11.8 5.9 %copy-start.5 = (f32[4]{0:T(128)S(1)}, f32[4]{0:T(128)}, u32[]{:S(2)}) copy-start(f32[4]{0:T(128)} %param.19) | copy-start | bytes 52
  11.8 5.9 %copy-start.6 = (f32[16]{0:T(128)S(1)}, f32[16]{0:T(128)}, u32[]{:S(2)}) copy-start(f32[16]{0:T(128)} %param.18) | copy-start | bytes 196
  11.8 291.1 %copy-start.2 = (f32[1,512]{1,0:T(1,128)S(1)}, f32[1,512]{1,0:T(1,128)}, u32[]{:S(2)}) copy-start(f32[1,512]{1,0:T(1,128)} %mean_ref.3) | copy-start | bytes 6148
  303.0 1.6 copy-start
Sparse Core Ops, SparseCore 0:
  17.8 285.0 all-reduce.3

commit v2 on v1

v2 whole, which is shorter than its diff:
```python
import jax
import jax.numpy as jnp
from jax import lax
from jax.experimental import pallas as pl
from jax.experimental.pallas import tpu as pltpu
from jax.sharding import Mesh
from jax.sharding import PartitionSpec as P

MEMBERS = 80
TX = 16
TY = 32
NBATCH = 6
PROWS = 8
NPATCH = 128
NLEV = 4
BIN = 16
CAP = 24
NOBS = 1024
CELLS = TX * TY
UNIT = NBATCH * CAP
WIDE = 128
TILE = 512
SPAN = 256
LIVE_COLS = NBATCH * NOBS
COLS = LIVE_COLS + CELLS
INNOV, VAR, POS_X, POS_Y, POS_Z = 80, 83, 86, 87, 88
VMEM = pltpu.VMEM
SMEM = pltpu.SMEM
F32 = jnp.float32
BF16 = jnp.bfloat16


def split3(value):
    high = value.astype(BF16).astype(F32)
    mid = (value - high).astype(BF16).astype(F32)
    return high, mid, value - high - mid


def select_kernel(where_ref, order_ref, count_ref, cell_ref, lev_ref, value_ref, var_ref, pert_ref, mean_ref, out_ref):
    patch = where_ref[0]
    level = where_ref[1]
    window = jnp.minimum(patch * CAP // WIDE, NPATCH * CAP // WIDE - 2)
    shift = lax.rem(2 * WIDE - (patch * CAP - window * WIDE), 2 * WIDE)
    start = pl.multiple_of(window * WIDE, WIDE)

    def column(ref):
        rows = pltpu.roll(ref[:, pl.ds(start, 2 * WIDE)].astype(F32), shift, 1)[:, :WIDE]
        wide = jnp.concatenate([rows, jnp.zeros((WIDE - 8, WIDE), F32)], axis=0).T[:, :8]
        lane = lax.broadcasted_iota(jnp.int32, (CAP, 8), 1)
        wide = wide[:CAP]
        return jnp.concatenate(
            [jnp.sum(jnp.where(lane == order_ref[k], wide, 0.0), axis=1, keepdims=True) for k in range(NBATCH)], axis=0
        )

    slot = lax.broadcasted_iota(jnp.int32, (CAP, 1), 0)
    live = jnp.concatenate(
        [(slot < count_ref[order_ref[k], patch]).astype(F32) for k in range(NBATCH)], axis=0
    )
    cell, lev, value, var = column(cell_ref), column(lev_ref), column(value_ref), column(var_ref)
    own = (live > 0.5) & (lev == level.astype(F32))
    mean_parts = split3(mean_ref[...])
    source = jnp.concatenate([pert_ref[...], *mean_parts, jnp.zeros((WIDE - 83, CELLS), F32)], axis=0).astype(BF16)
    spot = lax.broadcasted_iota(jnp.int32, (UNIT, CELLS), 1)
    hot = jnp.where((spot == cell.astype(jnp.int32)) & own, 1.0, 0.0).astype(BF16)
    taken = lax.dot_general(hot, source, (((1,), (1,)), ((), ())), preferred_element_type=F32)
    innov = value - (taken[:, 80:81] + taken[:, 81:82] + taken[:, 82:83])
    across = (cell * (1.0 / TY)).astype(jnp.int32).astype(F32)
    obs_x = across + (patch // PROWS * TX).astype(F32)
    obs_y = cell - across * TY + (patch % PROWS * TY).astype(F32)
    lane = lax.broadcasted_iota(jnp.int32, (UNIT, WIDE), 1)
    out = jnp.where(lane < MEMBERS, taken, 0.0)
    for at, item in enumerate([*split3(innov), *split3(var), obs_x, obs_y, lev]):
        out = jnp.where(lane == INNOV + at, item, out)
    out_ref[...] = jnp.where(own, out, 0.0).astype(BF16)


def filter_kernel(
    where_ref,
    order_ref,
    count_ref,
    vert_ref,
    horiz_ref,
    got_ref,
    pert_ref,
    mean_ref,
    post_pert_ref,
    post_mean_ref,
    state,
    hot_x,
    hot_y,
    dist,
    tab_x,
    tab_y,
    levw,
):
    patch = where_ref[0]
    level = where_ref[1].astype(F32)

    for k in range(NBATCH):
        skip = (k % 2) * 8

        def place(p, first, k=k, skip=skip):
            rows = got_ref[pl.ds(pl.multiple_of(p * UNIT + k * CAP - skip, 16), 32), :].astype(F32)
            state[pl.ds(k * NOBS + first, CAP), :] = rows[skip : skip + CAP]
            return first + count_ref[order_ref[k], p]

        lax.fori_loop(0, NPATCH, place, 0, unroll=4)
    own = jnp.concatenate(
        [pert_ref[...], -mean_ref[...], jnp.zeros((WIDE - 81, CELLS), F32)], axis=0
    )
    state[LIVE_COLS:COLS, :] = own.T

    def mark(t, unused):
        at = pl.multiple_of(t * TILE, TILE)
        rows = state[pl.ds(at, TILE), :]
        lane = lax.broadcasted_iota(jnp.int32, (TILE, SPAN), 1).astype(F32)
        hot_x[pl.ds(at, TILE), :] = jnp.where(lane == rows[:, POS_X : POS_X + 1], 1.0, 0.0).astype(BF16)
        hot_y[pl.ds(at, TILE), :] = jnp.where(lane == rows[:, POS_Y : POS_Y + 1], 1.0, 0.0).astype(BF16)
        return unused

    lax.fori_loop(0, LIVE_COLS // TILE, mark, 0)

    def lookup(bins):
        table = jnp.broadcast_to(horiz_ref[...], (bins.shape[0], WIDE))
        parts = [
            jnp.take_along_axis(table, bins[:, j : j + WIDE], axis=1) for j in range(0, bins.shape[1], WIDE)
        ]
        return jnp.concatenate(parts, axis=1)

    def bins_x(one, other):
        apart = jnp.abs(one - other)
        return (jnp.minimum(apart, SPAN - apart) * (1.0 / BIN)).astype(jnp.int32)

    def bins_y(one, other):
        return (jnp.abs(one - other) * (1.0 / BIN)).astype(jnp.int32)

    one = lax.broadcasted_iota(jnp.int32, (SPAN, SPAN), 0).astype(F32)
    other = lax.broadcasted_iota(jnp.int32, (SPAN, SPAN), 1).astype(F32)
    for at, bins in enumerate((bins_x(one, other), bins_y(one, other))):
        value = lookup(bins)
        high = value.astype(BF16)
        dist[2 * at] = high
        dist[2 * at + 1] = (value - high.astype(F32)).astype(BF16)

    def vertical(apart):
        found = jnp.zeros_like(apart)
        for step in range(NLEV):
            found = jnp.where(apart == float(step), vert_ref[step], found)
        return found

    def batch(k, unused):
        start = pl.multiple_of(k * NOBS, NOBS)
        block = state[pl.ds(start, NOBS), :].T
        innov = block[INNOV : INNOV + 1] + block[INNOV + 1 : INNOV + 2] + block[INNOV + 2 : INNOV + 3]
        obs_var = block[VAR : VAR + 1] + block[VAR + 1 : VAR + 2] + block[VAR + 2 : VAR + 3]
        obs_x, obs_y, obs_z = block[POS_X : POS_X + 1], block[POS_Y : POS_Y + 1], block[POS_Z : POS_Z + 1]
        row = lax.broadcasted_iota(jnp.int32, (WIDE, NOBS), 0)
        prior = jnp.where(row < MEMBERS, block, 0.0).astype(BF16)
        values = prior.astype(F32)
        spread = jnp.sum(values * values, axis=0, keepdims=True) / (MEMBERS - 1.0) + obs_var
        shrink = 1.0 / (1.0 + jnp.sqrt(obs_var / spread))
        scale = 1.0 / ((MEMBERS - 1.0) * spread)
        coeffs = jnp.where(row == MEMBERS, innov.astype(BF16).astype(F32), values * shrink).T.astype(BF16)

        own_a = lax.broadcasted_iota(jnp.int32, (TX, NOBS), 0) + patch // PROWS * TX
        own_e = lax.broadcasted_iota(jnp.int32, (TY, NOBS), 0) + patch % PROWS * TY
        weight_x = lookup(bins_x(own_a.astype(F32), obs_x)) * (vertical(jnp.abs(obs_z - level)) * scale)
        weight_y = lookup(bins_y(own_e.astype(F32), obs_y))
        cells = state[LIVE_COLS:COLS, :]
        lhs = cells.astype(BF16)
        change = jnp.zeros((CELLS, WIDE), F32)
        for j in range(0, NOBS, SPAN):
            part = slice(j, j + SPAN)
            cov = jnp.dot(lhs, prior[:, part], preferred_element_type=F32)
            gain = jnp.concatenate(
                [
                    (cov[a * TY : (a + 1) * TY] * (weight_x[a : a + 1, part] * weight_y[:, part])).astype(BF16)
                    for a in range(TX)
                ],
                axis=0,
            )
            change = change + jnp.dot(gain, coeffs[part], preferred_element_type=F32)
        state[LIVE_COLS:COLS, :] = cells - change

        @pl.when(k < NBATCH - 1)
        def _():
            root = jnp.sqrt(scale)
            contract = (((1,), (1,)), ((), ()))
            for tab, hot, at in ((tab_x, hot_x, 0), (tab_y, hot_y, 2)):
                here = hot[pl.ds(start, NOBS), :]
                full = lax.dot_general(dist[at], here, contract, preferred_element_type=F32)
                full = full + lax.dot_general(dist[at + 1], here, contract, preferred_element_type=F32)
                tab[...] = (full * root).astype(BF16)
            for z in range(NLEV):
                levw[z : z + 1, :] = vertical(jnp.abs(obs_z - float(z)))

        def tile(t, unused):
            at = pl.multiple_of(t * TILE, TILE)
            cells = state[pl.ds(at, TILE), :]
            lhs = cells.astype(BF16)
            lhs_x = hot_x[pl.ds(at, TILE), :]
            lhs_y = hot_y[pl.ds(at, TILE), :]
            cell_z = jnp.broadcast_to(cells[:, POS_Z : POS_Z + 1], (TILE, SPAN))
            change = jnp.zeros((TILE, WIDE), F32)
            for j in range(0, NOBS, SPAN):
                part = slice(j, j + SPAN)
                cov = jnp.dot(lhs, prior[:, part], preferred_element_type=F32)
                near = jnp.dot(lhs_x, tab_x[:, part], preferred_element_type=F32)
                far = jnp.dot(lhs_y, tab_y[:, part], preferred_element_type=F32)
                high = jnp.where(cell_z == 2.0, levw[2:3, part], levw[3:4, part])
                up = jnp.where(cell_z == 0.0, levw[0:1, part], jnp.where(cell_z == 1.0, levw[1:2, part], high))
                gain = (near * far * (cov * up)).astype(BF16)
                change = change + jnp.dot(gain, coeffs[part], preferred_element_type=F32)
            state[pl.ds(at, TILE), :] = cells - change
            return unused

        return lax.fori_loop((k + 1) * (NOBS // TILE), LIVE_COLS // TILE, tile, unused)

    lax.fori_loop(0, NBATCH, batch, 0)
    block = state[LIVE_COLS:COLS, :].T
    post_pert_ref[...] = block[:MEMBERS]
    post_mean_ref[...] = -block[MEMBERS : MEMBERS + 1]


def select_call(where, order, count, cell, lev, value, var, pert, mean):
    return pl.pallas_call(
        select_kernel,
        out_shape=jax.ShapeDtypeStruct((UNIT, WIDE), BF16),
        in_specs=[pl.BlockSpec(memory_space=SMEM)] * 3 + [pl.BlockSpec(memory_space=VMEM)] * 6,
        out_specs=pl.BlockSpec(memory_space=VMEM),
        compiler_params=pltpu.CompilerParams(vmem_limit_bytes=48 << 20),
    )(where, order, count, cell, lev, value, var, pert, mean)


def filter_call(where, order, count, vert, horiz, got, pert, mean):
    return pl.pallas_call(
        filter_kernel,
        out_shape=(
            jax.ShapeDtypeStruct((MEMBERS, CELLS), F32),
            jax.ShapeDtypeStruct((1, CELLS), F32),
        ),
        in_specs=[pl.BlockSpec(memory_space=SMEM)] * 4 + [pl.BlockSpec(memory_space=VMEM)] * 4,
        out_specs=(pl.BlockSpec(memory_space=VMEM),) * 2,
        scratch_shapes=[
            VMEM((COLS, WIDE), F32),
            VMEM((LIVE_COLS, SPAN), BF16),
            VMEM((LIVE_COLS, SPAN), BF16),
            VMEM((4, SPAN, SPAN), BF16),
            VMEM((SPAN, NOBS), BF16),
            VMEM((SPAN, NOBS), BF16),
            VMEM((8, NOBS), F32),
        ],
        compiler_params=pltpu.CompilerParams(vmem_limit_bytes=56 << 20),
    )(where, order, count, vert, horiz, got, pert, mean)


AXES = ("y_hi", "x", "z", "core")


def shards(
    prior_mean,
    prior_pert,
    obs_value,
    obs_var,
    obs_cell,
    obs_level,
    obs_count,
    batch_order,
    horiz_weight,
    vert_weight,
):
    where = jnp.stack([lax.axis_index(AXES), lax.axis_index("y_lo")]).astype(jnp.int32)
    pert = prior_pert.reshape(MEMBERS, CELLS)
    mean = prior_mean.reshape(1, CELLS)
    mine = select_call(where, batch_order, obs_count, obs_cell, obs_level, obs_value, obs_var, pert, mean)
    others = [
        lax.ppermute(mine, "y_lo", [(i, (i + step) % NLEV) for i in range(NLEV)]) for step in range(1, NLEV)
    ]
    for other in others:
        mine = mine + other
    got = lax.all_gather(mine, AXES, axis=0, tiled=True)
    horiz = jnp.pad(horiz_weight[None, :], ((0, 0), (0, WIDE - horiz_weight.shape[0])))
    post_pert, post_mean = filter_call(where, batch_order, obs_count, vert_weight, horiz, got, pert, mean)
    return post_mean.reshape(prior_mean.shape), post_pert.reshape(prior_pert.shape)


def solution(mesh):
    whole = Mesh(mesh.devices.reshape(2, 4, 8, 2, NLEV), AXES + ("y_lo",))
    return jax.shard_map(
        shards,
        mesh=whole,
        in_specs=(
            P("y_lo", AXES),
            P(None, "y_lo", AXES),
            P(),
            P(),
            P(),
            P(),
            P(),
            P(),
            P(),
            P(),
        ),
        out_specs=(P("y_lo", AXES), P(None, "y_lo", AXES)),
        check_vma=False,
    )
```

time: 447 us -> 249 us (0.56)
  waiting for transfers between devices: 285 us -> 148 us
  Pallas kernels: 140 us -> 66 us
  starting transfers between devices: 0.04 us -> 10.4 us
    psum x1 -> x0, waiting for transfers between devices: 285 us -> none  [shards(): obs = lax.psum(obs, ('patch', 'lev'))]
    all_gather x0 -> x1, waiting for transfers between devices: none -> 144 us  [shards(): got = lax.all_gather(mine, AXES, axis=0, tiled=True)]
    pallas_call x2, Pallas kernels: 140 us -> 66 us  [the longest x1 64.5 us: filter_call(): pl.pallas_call(filter_kernel, out_shape=(jax.ShapeDtypeStruct((MEMBERS, C...]
    ppermute x0 -> x3, starting transfers between devices: none -> 10.3 us  [shards(): lax.ppermute(mine, 'y_lo', [(i, (i + step) % NLEV) for i in range(NLEV)])]
  transfers between devices with their start and end apart: 1 -> 4, of which waited for: 1 -> 3; matrix products, arithmetic and copies ran while one was open for 0% -> 0% of each run, Pallas kernels for 0% -> 0%
where the time goes in v2:
time: 249 us
  waiting for transfers between devices  148 us (59%)
  Pallas kernels  66 us (27%)
  between operations  14.1 us (6%)
  starting transfers between devices  10.4 us (4%)
  local copies, waits for them, and re-layouts  9.48 us (4%)
    all_gather x1, waiting for transfers between devices, shards(): got = lax.all_gather(mine, AXES, axis=0, tiled=True)  144 us
    pallas_call x1, Pallas kernels, filter_call(): pl.pallas_call(filter_kernel, out_shape=(jax.ShapeDtypeStruct((MEMBERS, C...  64.5 us
    ppermute x3, starting transfers between devices, shards(): lax.ppermute(mine, 'y_lo', [(i, (i + step) % NLEV) for i in range(NLEV)])  10.3 us
    unnamed x20, local copies, waits for them, and re-layouts  8.28 us
  transfers between devices with their start and end apart: 4, of which 3 were waited for; matrix products, arithmetic and copies ran while one was open for 0% of the time, Pallas kernels for 0%

profile of v2, /device:TPU:1, one launch (start us, length us, event | category | flops | bytes accessed | tf_op | source)
XLA Modules:
  0.0 249.1 jit_solution(3774789619938526053)
XLA Ops:
  7.2 0.0 all-gather.2.cloned.1.call-start
  7.2 0.9 copy.15
  8.1 0.0 copy-start
  8.2 0.1 pad_add_fusion.where_ref
  8.3 0.9 copy-done.1
  9.2 0.9 copy-done.2
  10.0 0.9 copy-done.3
  10.9 0.9 copy-done.4
  11.8 0.7 copy-done.5
  12.5 0.7 copy-done.6
  13.2 0.7 copy-done.7
  13.9 1.5 shard_map.113
  15.4 6.1 %collective-permute-start.2 = (bf16[144,128]{1,0:T(8,128)(2,1)S(1)}, bf16[144,128]{1,0:T(8,128)(2,1)S(1)}, u32[]{:S(2)}, u32[]{:S(2)}) collective-permute-start(bf16[144,128]{1,0:T(8,128)(2,1)S(1)} %shard_map.113), channel_id=1, source_target_pairs={{0,3},{1,0},{2,1},{3,2},{4,7},{5,4},{6,5},{7,6},{8,11},{9,8},{10,9... | collective-permute-start | bytes 110600 | tf_op jit(solution)/shard_map/ppermute | solution.py:277
  21.4 1.9 collective-permute-start.1
  23.4 2.3 collective-permute-start
  25.7 0.0 collective-permute-done.2
  25.7 1.3 collective-permute-done.1
  27.0 2.8 %collective-permute-done = bf16[144,128]{1,0:T(8,128)(2,1)S(1)} collective-permute-done((bf16[144,128]{1,0:T(8,128)(2,1)S(1)}, bf16[144,128]{1,0:T(8,128)(2,1)S(1)}, u32[]{:S(2)}, u32[]{:S(2)}) %collective-permute-start) | collective-permute-done | bytes 36896 | tf_op jit(solution)/shard_map/ppermute | solution.py:277
  29.9 0.6 add_add_fusion
  30.5 0.0 all-gather.2.cloned.1.call-update
  30.5 1.2 pad.4.horiz_ref
  31.7 144.2 %all-gather.2.cloned.1.call-done.got_ref = bf16[18432,128]{1,0:T(8,128)(2,1)} async-done(((bf16[144,128]{1,0:T(8,128)(2,1)}), bf16[18432,128]{1,0:T(8,128)(2,1)}) %all-gather.2.cloned.1.call-update) | async-done | bytes 4718608 | tf_op jit(solution)/shard_map/all_gather | solution.py:281
  175.9 64.5 %shard_map.114 = (f32[80,512]{1,0:T(8,128)}, f32[1,512]{1,0:T(1,128)}) custom-call(s32[2]{0:T(128)} %copy-done.8, s32[8]{0:T(128)} %order_ref.3, s32[8,128]{1,0:T(8,128)} %count_ref.3, f32[4]{0:T(128)} %vert_ref.1, f32[1,128]{1,0:T(1,128)} %pad.4.horiz_ref, bf16[18432,128]{1,0:T(8,128)(2,1)} %all-gather.2.cloned.1.call-done.got_ref, f32[80,512]{1,0:T(8,128)} %bitcast.8, ...), custom_call_target="tpu_custom_call" | custom-call | tf_op jit(solution)/shard_map/pallas_call | solution.py:236
  240.5 1.8 copy.12
  (10 shorter events, 0.0 us)
Async XLA Ops:
  7.2 168.8 %all-gather.2.cloned.1.call-start = ((), (), s32[]{:S(2)}) async-start(), calls=%async_computation | async-start | bytes 4755456 | tf_op jit(solution)/shard_map/all_gather | solution.py:281
  8.1 167.8 %copy-start = (f32[80,1,512]{2,0,1:T(8,128)}, f32[80,1,512]{2,0,1:T(8,128)S(1)}, u32[]{:S(2)}) copy-start(f32[80,1,512]{2,0,1:T(8,128)S(1)} %copy.15) | copy-start | bytes 491524
  8.3 167.7 %copy-start.8 = (s32[2]{0:T(128)}, s32[2]{0:T(128)S(1)}, u32[]{:S(2)}) copy-start(s32[2]{0:T(128)S(1)} %pad_add_fusion.where_ref) | copy-start | bytes 28
  8.3 0.9 copy-start.1
  9.2 0.9 copy-start.2
  10.0 0.9 copy-start.3
  10.9 0.9 copy-start.4
  11.8 0.7 copy-start.5
  12.5 0.7 copy-start.6
  13.2 0.7 copy-start.7
  15.4 10.4 %collective-permute-start.2 = (bf16[144,128]{1,0:T(8,128)(2,1)S(1)}, bf16[144,128]{1,0:T(8,128)(2,1)S(1)}, u32[]{:S(2)}, u32[]{:S(2)}) collective-permute-start(bf16[144,128]{1,0:T(8,128)(2,1)S(1)} %shard_map.113), channel_id=1, source_target_pairs={{0,3},{1,0},{2,1},{3,2},{4,7},{5,4},{6,5},{7,6},{8,11},{9,8},{10,9... | collective-permute-start | bytes 110600 | tf_op jit(solution)/shard_map/ppermute | solution.py:277
  21.4 5.6 %collective-permute-start.1 = (bf16[144,128]{1,0:T(8,128)(2,1)S(1)}, bf16[144,128]{1,0:T(8,128)(2,1)S(1)}, u32[]{:S(2)}, u32[]{:S(2)}) collective-permute-start(bf16[144,128]{1,0:T(8,128)(2,1)S(1)} %shard_map.113), channel_id=1, source_target_pairs={{0,2},{1,3},{2,0},{3,1},{4,6},{5,7},{6,4},{7,5},{8,10},{9,11},{10,... | collective-permute-start | bytes 110600 | tf_op jit(solution)/shard_map/ppermute | solution.py:277
  23.4 6.5 %collective-permute-start = (bf16[144,128]{1,0:T(8,128)(2,1)S(1)}, bf16[144,128]{1,0:T(8,128)(2,1)S(1)}, u32[]{:S(2)}, u32[]{:S(2)}) collective-permute-start(bf16[144,128]{1,0:T(8,128)(2,1)S(1)} %shard_map.113), channel_id=1, source_target_pairs={{0,1},{1,2},{2,3},{3,0},{4,5},{5,6},{6,7},{7,4},{8,9},{9,10},{10,1... | collective-permute-start | bytes 110600 | tf_op jit(solution)/shard_map/ppermute | solution.py:277
Sparse Core Ops, SparseCore 0:
  30.6 145.2 all-gather.1

commit v3 on v2

--- a/solution.py
+++ b/solution.py
@@ -102,7 +102,8 @@
         def place(p, first, k=k, skip=skip):
             rows = got_ref[pl.ds(pl.multiple_of(p * UNIT + k * CAP - skip, 16), 32), :].astype(F32)
             state[pl.ds(k * NOBS + first, CAP), :] = rows[skip : skip + CAP]
-            return first + count_ref[order_ref[k], p]
+            z, y_hi, core, x = p % 8, p // 8 % 2, p // 16 % 2, p // 32
+            return first + count_ref[order_ref[k], ((y_hi * 4 + x) * 8 + z) * 2 + core]
 
         lax.fori_loop(0, NPATCH, place, 0, unroll=4)
     own = jnp.concatenate(
@@ -273,12 +274,10 @@
     pert = prior_pert.reshape(MEMBERS, CELLS)
     mean = prior_mean.reshape(1, CELLS)
     mine = select_call(where, batch_order, obs_count, obs_cell, obs_level, obs_value, obs_var, pert, mean)
-    others = [
-        lax.ppermute(mine, "y_lo", [(i, (i + step) % NLEV) for i in range(NLEV)]) for step in range(1, NLEV)
-    ]
-    for other in others:
-        mine = mine + other
-    got = lax.all_gather(mine, AXES, axis=0, tiled=True)
+    for step in (1, 2):
+        mine = mine + lax.ppermute(mine, "y_lo", [(i, i ^ step) for i in range(NLEV)])
+    group = lax.all_gather(mine, ("y_hi", "z"), axis=0, tiled=True)
+    got = lax.all_gather(group, ("x", "core"), axis=0, tiled=True)
     horiz = jnp.pad(horiz_weight[None, :], ((0, 0), (0, WIDE - horiz_weight.shape[0])))
     post_pert, post_mean = filter_call(where, batch_order, obs_count, vert_weight, horiz, got, pert, mean)
     return post_mean.reshape(prior_mean.shape), post_pert.reshape(prior_pert.shape)

time: 249 us -> 213 us (0.86)
  waiting for transfers between devices: 148 us -> 41.5 us
  blocking collectives: 0 us -> 59.7 us
  Pallas kernels: 66 us -> 78.6 us
    all_gather x1, waiting for transfers between devices: 144 us -> 38.8 us  [shards(): got = lax.all_gather(group, ('x', 'core'), axis=0, tiled=True)]
    all_gather x0 -> x1, blocking collectives: none -> 59.7 us  [shards(): group = lax.all_gather(mine, ('y_hi', 'z'), axis=0, tiled=True)]
    pallas_call x1, Pallas kernels: 64.5 us -> 77.1 us  [filter_call(): pl.pallas_call(filter_kernel, out_shape=(jax.ShapeDtypeStruct((MEMBERS, C...]
    ppermute x3 -> x2, starting transfers between devices: 10.3 us -> 8.41 us  [shards(): lax.ppermute(mine, 'y_lo', [(i, i ^ step) for i in range(NLEV)])]
  transfers between devices with their start and end apart: 4 -> 3, of which waited for: 3 -> 3; matrix products, arithmetic and copies ran while one was open for 0% -> 1% of each run, Pallas kernels for 0% -> 0%
where the time goes in v3:
time: 213 us; the launch traced here: 212 us
  Pallas kernels  78.6 us (37%)
  blocking collectives  59.7 us (28%)
  waiting for transfers between devices  41.5 us (19%)
  between operations  14.1 us (7%)
  local copies, waits for them, and re-layouts  9.53 us (4%)
  starting transfers between devices  8.44 us (4%)
    pallas_call x1, Pallas kernels, filter_call(): pl.pallas_call(filter_kernel, out_shape=(jax.ShapeDtypeStruct((MEMBERS, C...  77.1 us
    all_gather x1, blocking collectives, shards(): group = lax.all_gather(mine, ('y_hi', 'z'), axis=0, tiled=True)  59.7 us
    all_gather x1, waiting for transfers between devices, shards(): got = lax.all_gather(group, ('x', 'core'), axis=0, tiled=True)  38.8 us
    ppermute x2, starting transfers between devices, shards(): lax.ppermute(mine, 'y_lo', [(i, i ^ step) for i in range(NLEV)])  8.41 us
    unnamed x20, local copies, waits for them, and re-layouts  8.28 us
  transfers between devices with their start and end apart: 3, of which 3 were waited for; matrix products, arithmetic and copies ran while one was open for 1% of the time, Pallas kernels for 0%

profile of v3, /device:TPU:1, one launch (start us, length us, event | category | flops | bytes accessed | tf_op | source)
XLA Modules:
  0.0 212.1 jit_solution(12638723601961783367)
XLA Ops:
  7.2 0.0 all-gather.2.cloned.1.call-start
  7.2 0.9 copy.15
  8.1 0.0 copy-start
  8.2 0.1 pad_add_fusion.where_ref
  8.3 0.9 copy-done.1
  9.2 0.9 copy-done.2
  10.0 0.9 copy-done.3
  10.9 0.9 copy-done.4
  11.8 0.7 copy-done.5
  12.5 0.7 copy-done.6
  13.2 0.7 copy-done.7
  13.9 1.5 shard_map.113
  15.4 4.0 %collective-permute-start = (bf16[144,128]{1,0:T(8,128)(2,1)S(1)}, bf16[144,128]{1,0:T(8,128)(2,1)S(1)}, u32[]{:S(2)}, u32[]{:S(2)}) collective-permute-start(bf16[144,128]{1,0:T(8,128)(2,1)S(1)} %shard_map.113), channel_id=1, source_target_pairs={{0,1},{1,0},{2,3},{3,2},{4,5},{5,4},{6,7},{7,6},{8,9},{9,8},{10,11... | collective-permute-start | bytes 110600 | tf_op jit(solution)/shard_map/ppermute | solution.py:278
  19.4 1.3 collective-permute-done
  20.8 4.4 %collective-permute-start.1 = (bf16[144,128]{1,0:T(8,128)(2,1)S(1)}, bf16[144,128]{1,0:T(8,128)(2,1)S(1)}, u32[]{:S(2)}, u32[]{:S(2)}) collective-permute-start(bf16[144,128]{1,0:T(8,128)(2,1)S(1)} %add.20), channel_id=1, source_target_pairs={{0,2},{1,3},{2,0},{3,1},{4,6},{5,7},{6,4},{7,5},{8,10},{9,11},{10,... | collective-permute-start | bytes 110600 | tf_op jit(solution)/shard_map/ppermute | solution.py:278
  25.2 1.3 collective-permute-done.1
  26.5 59.7 %all_gather.6 = bf16[2304,128]{1,0:T(8,128)(2,1)} all-gather(bf16[144,128]{1,0:T(8,128)(2,1)S(1)} %add.21), channel_id=1, replica_groups=mesh['y_hi'=2,'x'=4,'z'=8,'core'=2,'y_lo'=4] {'y_hi','z'}, dimensions={0}, use_global_device_ids=true | all-gather | bytes 626688 | tf_op jit(solution)/shard_map/all_gather | solution.py:279
  86.2 0.0 all-gather.2.cloned.1.call-update
  86.3 1.2 pad.4.horiz_ref
  87.5 38.8 %all-gather.2.cloned.1.call-done.got_ref = bf16[18432,128]{1,0:T(8,128)(2,1)} async-done(((bf16[2304,128]{1,0:T(8,128)(2,1)}), bf16[18432,128]{1,0:T(8,128)(2,1)}) %all-gather.2.cloned.1.call-update) | async-done | bytes 4718608 | tf_op jit(solution)/shard_map/all_gather | solution.py:280
  126.4 0.0 copy-done
  126.4 0.0 copy-done.8
  126.4 77.1 %shard_map.114 = (f32[80,512]{1,0:T(8,128)}, f32[1,512]{1,0:T(1,128)}) custom-call(s32[2]{0:T(128)} %copy-done.8, s32[8]{0:T(128)} %order_ref.3, s32[8,128]{1,0:T(8,128)} %count_ref.3, f32[4]{0:T(128)} %vert_ref.1, f32[1,128]{1,0:T(1,128)} %pad.4.horiz_ref, bf16[18432,128]{1,0:T(8,128)(2,1)} %all-gather.2.cloned.1.call-done.got_ref, f32[80,512]{1,0:T(8,128)} %bitcast.8, ...), custom_call_target="tpu_custom_call" | custom-call | tf_op jit(solution)/shard_map/pallas_call | solution.py:237
  203.5 1.8 copy.12
  (10 shorter events, 0.0 us)
Async XLA Ops:
  7.2 119.2 %all-gather.2.cloned.1.call-start = ((), (), s32[]{:S(2)}) async-start(), calls=%async_computation | async-start | bytes 5308416 | tf_op jit(solution)/shard_map/all_gather | solution.py:280
  8.1 118.2 %copy-start = (f32[80,1,512]{2,0,1:T(8,128)}, f32[80,1,512]{2,0,1:T(8,128)S(1)}, u32[]{:S(2)}) copy-start(f32[80,1,512]{2,0,1:T(8,128)S(1)} %copy.15) | copy-start | bytes 491524
  8.3 118.1 %copy-start.8 = (s32[2]{0:T(128)}, s32[2]{0:T(128)S(1)}, u32[]{:S(2)}) copy-start(s32[2]{0:T(128)S(1)} %pad_add_fusion.where_ref) | copy-start | bytes 28
  8.3 0.9 copy-start.1
  9.2 0.9 copy-start.2
  10.0 0.9 copy-start.3
  10.9 0.9 copy-start.4
  11.8 0.7 copy-start.5
  12.5 0.7 copy-start.6
  13.2 0.7 copy-start.7
  15.4 5.4 %collective-permute-start = (bf16[144,128]{1,0:T(8,128)(2,1)S(1)}, bf16[144,128]{1,0:T(8,128)(2,1)S(1)}, u32[]{:S(2)}, u32[]{:S(2)}) collective-permute-start(bf16[144,128]{1,0:T(8,128)(2,1)S(1)} %shard_map.113), channel_id=1, source_target_pairs={{0,1},{1,0},{2,3},{3,2},{4,5},{5,4},{6,7},{7,6},{8,9},{9,8},{10,11... | collective-permute-start | bytes 110600 | tf_op jit(solution)/shard_map/ppermute | solution.py:278
  20.8 5.7 %collective-permute-start.1 = (bf16[144,128]{1,0:T(8,128)(2,1)S(1)}, bf16[144,128]{1,0:T(8,128)(2,1)S(1)}, u32[]{:S(2)}, u32[]{:S(2)}) collective-permute-start(bf16[144,128]{1,0:T(8,128)(2,1)S(1)} %add.20), channel_id=1, source_target_pairs={{0,2},{1,3},{2,0},{3,1},{4,6},{5,7},{6,4},{7,5},{8,10},{9,11},{10,... | collective-permute-start | bytes 110600 | tf_op jit(solution)/shard_map/ppermute | solution.py:278
Sparse Core Ops, SparseCore 0:
  86.4 39.9 all-gather.1

commit v4 on v3

v4 whole, which is shorter than its diff:
```python
import jax
import jax.numpy as jnp
from jax import lax
from jax.experimental import pallas as pl
from jax.experimental.pallas import tpu as pltpu
from jax.sharding import Mesh
from jax.sharding import PartitionSpec as P

MEMBERS = 80
TX = 16
TY = 32
NBATCH = 6
PROWS = 8
NPATCH = 128
NLEV = 4
BIN = 16
CAP = 24
NOBS = 1024
CELLS = TX * TY
UNIT = NBATCH * CAP
WIDE = 128
TILE = 512
SPAN = 256
LIVE_COLS = NBATCH * NOBS
COLS = LIVE_COLS + CELLS
NTILES = NBATCH * (NBATCH - 1) // 2 * (NOBS // TILE)
INNOV, VAR, POS_X, POS_Y, POS_Z = 80, 83, 86, 87, 88
VMEM = pltpu.VMEM
SMEM = pltpu.SMEM
F32 = jnp.float32
BF16 = jnp.bfloat16


def split3(value):
    high = value.astype(BF16).astype(F32)
    mid = (value - high).astype(BF16).astype(F32)
    return high, mid, value - high - mid


def select_kernel(
    where_ref,
    order_hbm,
    count_hbm,
    cell_hbm,
    lev_hbm,
    value_hbm,
    var_hbm,
    mean_hbm,
    pert_ref,
    out_ref,
    first_ref,
    order_ref,
    count_ref,
    count_all,
    cell_ref,
    lev_ref,
    value_ref,
    var_ref,
    mean_ref,
    sems,
):
    patch = where_ref[0]
    level = where_ref[1]
    window = jnp.minimum(patch * CAP // WIDE, NPATCH * CAP // WIDE - 2)
    shift = lax.rem(2 * WIDE - (patch * CAP - window * WIDE), 2 * WIDE)
    start = pl.multiple_of(window * WIDE, WIDE)
    near = pl.ds(start, 2 * WIDE)
    pairs = [
        (order_hbm, order_ref),
        (count_hbm, count_ref),
        (count_hbm, count_all),
        (cell_hbm.at[:, near], cell_ref),
        (lev_hbm.at[:, near], lev_ref),
        (value_hbm.at[:, near], value_ref),
        (var_hbm.at[:, near], var_ref),
        (mean_hbm, mean_ref),
    ]
    copies = [pltpu.make_async_copy(one, other, sems.at[i]) for i, (one, other) in enumerate(pairs)]
    for copy in copies:
        copy.start()
    for copy in copies:
        copy.wait()

    def column(ref):
        rows = pltpu.roll(ref[...].astype(F32), shift, 1)[:, :WIDE]
        wide = jnp.concatenate([rows, jnp.zeros((WIDE - 8, WIDE), F32)], axis=0).T[:, :8]
        lane = lax.broadcasted_iota(jnp.int32, (CAP, 8), 1)
        wide = wide[:CAP]
        return jnp.concatenate(
            [jnp.sum(jnp.where(lane == order_ref[k], wide, 0.0), axis=1, keepdims=True) for k in range(NBATCH)], axis=0
        )

    one = lax.broadcasted_iota(jnp.int32, (NPATCH, NPATCH), 0)
    other = lax.broadcasted_iota(jnp.int32, (NPATCH, NPATCH), 1)
    before = jnp.where(gathered(one) < gathered(other), 1.0, 0.0).astype(BF16)
    counts = count_all[...].astype(F32).astype(BF16)
    first_ref[...] = jnp.dot(counts, before, preferred_element_type=F32).astype(jnp.int32)

    slot = lax.broadcasted_iota(jnp.int32, (CAP, 1), 0)
    live = jnp.concatenate(
        [(slot < count_ref[order_ref[k], patch]).astype(F32) for k in range(NBATCH)], axis=0
    )
    cell, lev, value, var = column(cell_ref), column(lev_ref), column(value_ref), column(var_ref)
    own = (live > 0.5) & (lev == level.astype(F32))
    mean_parts = split3(mean_ref[...])
    source = jnp.concatenate([pert_ref[...], *mean_parts, jnp.zeros((WIDE - 83, CELLS), F32)], axis=0).astype(BF16)
    spot = lax.broadcasted_iota(jnp.int32, (UNIT, CELLS), 1)
    hot = jnp.where((spot == cell.astype(jnp.int32)) & own, 1.0, 0.0).astype(BF16)
    taken = lax.dot_general(hot, source, (((1,), (1,)), ((), ())), preferred_element_type=F32)
    innov = value - (taken[:, 80:81] + taken[:, 81:82] + taken[:, 82:83])
    across = (cell * (1.0 / TY)).astype(jnp.int32).astype(F32)
    obs_x = across + (patch // PROWS * TX).astype(F32)
    obs_y = cell - across * TY + (patch % PROWS * TY).astype(F32)
    lane = lax.broadcasted_iota(jnp.int32, (UNIT, WIDE), 1)
    out = jnp.where(lane < MEMBERS, taken, 0.0)
    for at, item in enumerate([*split3(innov), *split3(var), obs_x, obs_y, lev]):
        out = jnp.where(lane == INNOV + at, item, out)
    out = jnp.where(own, out, 0.0).astype(BF16)
    for z in range(NLEV):
        out_ref[z] = out


def gathered(patch):
    return (((patch >> 4) & 3) * 2 + (patch & 1)) * 16 + (patch >> 6) * 8 + ((patch >> 1) & 7)


def spots(g):
    x, core, y_hi = g // 4, g // 2 % 2, g % 2
    return y_hi * 64 + x * 16 + core, g * 8


def first_tile(k):
    return (k + 1) * (NOBS // TILE)


def taper_kernel(
    order_ref, first_ref, vert_ref, horiz_ref, cell_ref, lev_ref, out_hbm, code_ref, slots, place, dist, tab_x, tab_y, levw, bufs, sems
):
    spot = lax.broadcasted_iota(jnp.int32, (8, NPATCH * CAP), 1).astype(F32)
    patch = ((spot + 0.5) * (1.0 / CAP)).astype(jnp.int32)
    cell = cell_ref[...]
    at_x = (patch // PROWS) * TX + cell // TY
    at_y = (patch % PROWS) * TY + cell % TY
    code_ref[...] = (at_x * 1024 + at_y * NLEV + lev_ref[...]).astype(F32)

    def compact(k, unused):
        row = code_ref[pl.ds(order_ref[k], 1), :]
        for c in range(NPATCH * CAP // WIDE):
            part = slice(c * WIDE, (c + 1) * WIDE)
            slots[part, :] = jnp.broadcast_to(row[:, part], (WIDE, WIDE)).T
        pick = order_ref[k]

        def put(g, unused):
            patch0, row0 = spots(g)
            for z in range(8):
                p = patch0 + 2 * z
                rows = slots[pl.ds(pl.multiple_of(p * CAP, 8), CAP), :]
                place[pl.ds(k * NOBS + first_ref[pick, p], CAP), :] = rows
            return unused

        return lax.fori_loop(0, NPATCH // 8, put, unused)

    lax.fori_loop(0, NBATCH, compact, 0)

    def lookup(bins):
        table = jnp.broadcast_to(horiz_ref[...], (bins.shape[0], WIDE))
        parts = [
            jnp.take_along_axis(table, bins[:, j : j + WIDE], axis=1) for j in range(0, bins.shape[1], WIDE)
        ]
        return jnp.concatenate(parts, axis=1)

    one = lax.broadcasted_iota(jnp.int32, (SPAN, SPAN), 0)
    other = lax.broadcasted_iota(jnp.int32, (SPAN, SPAN), 1)
    apart = jnp.abs(one - other)
    for at, bins in enumerate((jnp.minimum(apart, SPAN - apart) // BIN, apart // BIN)):
        value = lookup(bins)
        high = value.astype(BF16)
        dist[2 * at] = high
        dist[2 * at + 1] = (value - high.astype(F32)).astype(BF16)

    def hot(index, rows):
        lane = lax.broadcasted_iota(jnp.int32, (rows, WIDE), 1)
        parts = [jnp.where(index - j == lane, 1.0, 0.0).astype(BF16) for j in range(0, SPAN, WIDE)]
        return jnp.concatenate(parts, axis=1)

    def out_copy(n):
        return pltpu.make_async_copy(bufs.at[n % 2], out_hbm.at[n], sems.at[n % 2])

    def batch(k, n):
        codes = place[pl.ds(pl.multiple_of(k * NOBS, NOBS), NOBS), :].astype(jnp.int32)
        obs_z = codes.astype(F32).T[:1].astype(jnp.int32) & 3
        lane = lax.broadcasted_iota(jnp.int32, (1, NOBS), 1)
        vary = 1.0 + (lane & 63).astype(F32) * (1.0 / 64.0)
        contract = (((1,), (1,)), ((), ()))
        for tab, index, at, factor in (
            (tab_x, codes >> 10, 0, vary),
            (tab_y, (codes >> 2) & 255, 2, 1.0 / vary),
        ):
            here = hot(index, NOBS)
            full = lax.dot_general(dist[at], here, contract, preferred_element_type=F32)
            full = full + lax.dot_general(dist[at + 1], here, contract, preferred_element_type=F32)
            tab[...] = (full * factor).astype(BF16)
        for z in range(NLEV):
            apart = jnp.abs(obs_z - z)
            found = jnp.zeros((1, NOBS), F32)
            for step in range(NLEV):
                found = jnp.where(apart == step, vert_ref[step], found)
            levw[z : z + 1, :] = found

        def tile(t, n):
            codes = place[pl.ds(pl.multiple_of(t * TILE, TILE), TILE), :].astype(jnp.int32)
            lhs_x = hot(codes >> 10, TILE)
            lhs_y = hot((codes >> 2) & 255, TILE)
            cell_z = codes & 3
            cell_z = jnp.concatenate([cell_z, cell_z], axis=1)

            @pl.when(n >= 2)
            def _():
                out_copy(n - 2).wait()

            buf = bufs.at[n % 2]
            for j in range(0, NOBS, SPAN):
                part = slice(j, j + SPAN)
                near = jnp.dot(lhs_x, tab_x[:, part], preferred_element_type=F32)
                far = jnp.dot(lhs_y, tab_y[:, part], preferred_element_type=F32)
                low = jnp.where(cell_z == 0, levw[0:1, part], levw[1:2, part])
                high = jnp.where(cell_z == 2, levw[2:3, part], levw[3:4, part])
                buf[:, part] = (near * far * jnp.where(cell_z < 2, low, high)).astype(BF16)
            out_copy(n).start()
            return n + 1

        return lax.fori_loop(first_tile(k), LIVE_COLS // TILE, tile, n)

    total = lax.fori_loop(0, NBATCH - 1, batch, 0)
    out_copy(total - 2).wait()
    out_copy(total - 1).wait()


def filter_kernel(
    where_ref,
    order_ref,
    first_ref,
    vert_ref,
    horiz_ref,
    got_ref,
    pert_ref,
    mean_ref,
    taper_hbm,
    post_pert_ref,
    post_mean_ref,
    state,
    bufs,
    sems,
):
    patch = where_ref[0]
    level = where_ref[1].astype(F32)

    def taper_copy(n):
        return pltpu.make_async_copy(taper_hbm.at[n], bufs.at[n % 2], sems.at[n % 2])

    taper_copy(0).start()

    for k in range(NBATCH):
        skip = (k % 2) * 8
        pick = order_ref[k]

        def place(g, unused, k=k, skip=skip, pick=pick):
            patch0, row0 = spots(g)
            for z in range(8):
                at = pl.multiple_of(row0 * UNIT + (z * UNIT + k * CAP - skip), 16)
                rows = got_ref[pl.ds(at, 32), :].astype(F32)
                state[pl.ds(k * NOBS + first_ref[pick, patch0 + 2 * z], CAP), :] = rows[skip : skip + CAP]
            return unused

        lax.fori_loop(0, NPATCH // 8, place, 0)
    own = jnp.concatenate(
        [pert_ref[...], -mean_ref[...], jnp.zeros((WIDE - 81, CELLS), F32)], axis=0
    )
    state[LIVE_COLS:COLS, :] = own.T

    def lookup(bins):
        table = jnp.broadcast_to(horiz_ref[...], (bins.shape[0], WIDE))
        parts = [
            jnp.take_along_axis(table, bins[:, j : j + WIDE], axis=1) for j in range(0, bins.shape[1], WIDE)
        ]
        return jnp.concatenate(parts, axis=1)

    def bins_x(one, other):
        apart = jnp.abs(one - other)
        return (jnp.minimum(apart, SPAN - apart) * (1.0 / BIN)).astype(jnp.int32)

    def bins_y(one, other):
        return (jnp.abs(one - other) * (1.0 / BIN)).astype(jnp.int32)

    def vertical(apart):
        found = jnp.zeros_like(apart)
        for step in range(NLEV):
            found = jnp.where(apart == float(step), vert_ref[step], found)
        return found

    def batch(k, n):
        start = pl.multiple_of(k * NOBS, NOBS)
        block = state[pl.ds(start, NOBS), :].T
        innov = block[INNOV : INNOV + 1] + block[INNOV + 1 : INNOV + 2] + block[INNOV + 2 : INNOV + 3]
        obs_var = block[VAR : VAR + 1] + block[VAR + 1 : VAR + 2] + block[VAR + 2 : VAR + 3]
        obs_x, obs_y, obs_z = block[POS_X : POS_X + 1], block[POS_Y : POS_Y + 1], block[POS_Z : POS_Z + 1]
        row = lax.broadcasted_iota(jnp.int32, (WIDE, NOBS), 0)
        prior = jnp.where(row < MEMBERS, block, 0.0).astype(BF16)
        values = prior.astype(F32)
        spread = jnp.sum(values * values, axis=0, keepdims=True) / (MEMBERS - 1.0) + obs_var
        shrink = 1.0 / (1.0 + jnp.sqrt(obs_var / spread))
        scale = 1.0 / ((MEMBERS - 1.0) * spread)
        coeffs = jnp.where(row == MEMBERS, innov.astype(BF16).astype(F32), values * shrink).T.astype(BF16)

        own_a = lax.broadcasted_iota(jnp.int32, (TX, NOBS), 0) + patch // PROWS * TX
        own_e = lax.broadcasted_iota(jnp.int32, (TY, NOBS), 0) + patch % PROWS * TY
        weight_x = lookup(bins_x(own_a.astype(F32), obs_x)) * (vertical(jnp.abs(obs_z - level)) * scale)
        weight_y = lookup(bins_y(own_e.astype(F32), obs_y))
        cells = state[LIVE_COLS:COLS, :]
        lhs = cells.astype(BF16)
        change = jnp.zeros((CELLS, WIDE), F32)
        for j in range(0, NOBS, SPAN):
            part = slice(j, j + SPAN)
            cov = jnp.dot(lhs, prior[:, part], preferred_element_type=F32)
            gain = jnp.concatenate(
                [
                    (cov[a * TY : (a + 1) * TY] * (weight_x[a : a + 1, part] * weight_y[:, part])).astype(BF16)
                    for a in range(TX)
                ],
                axis=0,
            )
            change = change + jnp.dot(gain, coeffs[part], preferred_element_type=F32)
        state[LIVE_COLS:COLS, :] = cells - change

        def tile(t, n):
            taper_copy(n).wait()

            @pl.when(n < NTILES - 1)
            def _():
                taper_copy(n + 1).start()

            at = pl.multiple_of(t * TILE, TILE)
            cells = state[pl.ds(at, TILE), :]
            lhs = cells.astype(BF16)
            taper = bufs.at[n % 2]
            change = jnp.zeros((TILE, WIDE), F32)
            for j in range(0, NOBS, SPAN):
                part = slice(j, j + SPAN)
                cov = jnp.dot(lhs, prior[:, part], preferred_element_type=F32)
                gain = (taper[:, part].astype(F32) * (cov * scale[:, part])).astype(BF16)
                change = change + jnp.dot(gain, coeffs[part], preferred_element_type=F32)
            state[pl.ds(at, TILE), :] = cells - change
            return n + 1

        return lax.fori_loop(first_tile(k), LIVE_COLS // TILE, tile, n)

    lax.fori_loop(0, NBATCH, batch, 0)
    block = state[LIVE_COLS:COLS, :].T
    post_pert_ref[...] = block[:MEMBERS]
    post_mean_ref[...] = -block[MEMBERS : MEMBERS + 1]


def select_call(where, order, count, cell, lev, value, var, mean, pert):
    return pl.pallas_call(
        select_kernel,
        out_shape=(
            jax.ShapeDtypeStruct((NLEV, UNIT, WIDE), BF16),
            jax.ShapeDtypeStruct((8, NPATCH), jnp.int32),
        ),
        in_specs=[pl.BlockSpec(memory_space=SMEM)]
        + [pl.BlockSpec(memory_space=pltpu.HBM)] * 7
        + [pl.BlockSpec(memory_space=VMEM)],
        out_specs=(pl.BlockSpec(memory_space=VMEM),) * 2,
        scratch_shapes=[
            SMEM((8,), jnp.int32),
            SMEM((8, NPATCH), jnp.int32),
            VMEM((8, NPATCH), jnp.int32),
            VMEM((8, 2 * WIDE), jnp.int32),
            VMEM((8, 2 * WIDE), jnp.int32),
            VMEM((8, 2 * WIDE), F32),
            VMEM((8, 2 * WIDE), F32),
            VMEM((1, CELLS), F32),
            pltpu.SemaphoreType.DMA((8,)),
        ],
        compiler_params=pltpu.CompilerParams(vmem_limit_bytes=60 << 20),
    )(where, order, count, cell, lev, value, var, mean, pert)


def taper_call(order, first, vert, horiz, cell, lev):
    return pl.pallas_call(
        taper_kernel,
        out_shape=jax.ShapeDtypeStruct((NTILES, TILE, NOBS), BF16),
        in_specs=[pl.BlockSpec(memory_space=SMEM)] * 3 + [pl.BlockSpec(memory_space=VMEM)] * 3,
        out_specs=pl.BlockSpec(memory_space=pltpu.HBM),
        scratch_shapes=[
            VMEM((8, NPATCH * CAP), F32),
            VMEM((NPATCH * CAP, WIDE), F32),
            VMEM((LIVE_COLS + 2 * CAP, WIDE), F32),
            VMEM((4, SPAN, SPAN), BF16),
            VMEM((SPAN, NOBS), BF16),
            VMEM((SPAN, NOBS), BF16),
            VMEM((8, NOBS), F32),
            VMEM((2, TILE, NOBS), BF16),
            pltpu.SemaphoreType.DMA((2,)),
        ],
        compiler_params=pltpu.CompilerParams(vmem_limit_bytes=48 << 20),
        cost_estimate=pl.CostEstimate(flops=2 * 15 * NOBS * NOBS * 512, bytes_accessed=32 << 20, transcendentals=0),
    )(order, first, vert, horiz, cell, lev)


def filter_call(where, order, first, vert, horiz, got, pert, mean, taper):
    return pl.pallas_call(
        filter_kernel,
        out_shape=(
            jax.ShapeDtypeStruct((MEMBERS, CELLS), F32),
            jax.ShapeDtypeStruct((1, CELLS), F32),
        ),
        in_specs=[pl.BlockSpec(memory_space=SMEM)] * 4
        + [pl.BlockSpec(memory_space=VMEM)] * 4
        + [pl.BlockSpec(memory_space=pltpu.HBM)],
        out_specs=(pl.BlockSpec(memory_space=VMEM),) * 2,
        scratch_shapes=[
            VMEM((COLS, WIDE), F32),
            VMEM((2, TILE, NOBS), BF16),
            pltpu.SemaphoreType.DMA((2,)),
        ],
        compiler_params=pltpu.CompilerParams(vmem_limit_bytes=48 << 20),
    )(where, order, first, vert, horiz, got, pert, mean, taper)


def exchange(block, axes):
    return lax.all_to_all(block, axes, 0, 0)


AXES = ("y_hi", "x", "z", "core")


def shards(
    prior_mean,
    prior_pert,
    obs_value,
    obs_var,
    obs_cell,
    obs_level,
    obs_count,
    batch_order,
    horiz_weight,
    vert_weight,
):
    where = jnp.stack([lax.axis_index(AXES), lax.axis_index("y_lo")]).astype(jnp.int32)
    pert = prior_pert.reshape(MEMBERS, CELLS)
    mean = prior_mean.reshape(1, CELLS)
    mine, first = select_call(where, batch_order, obs_count, obs_cell, obs_level, obs_value, obs_var, mean, pert)
    horiz = jnp.pad(horiz_weight[None, :], ((0, 0), (0, WIDE - horiz_weight.shape[0])))
    mine = jnp.sum(exchange(mine, "y_lo").astype(F32), axis=0).astype(BF16)
    group = exchange(jnp.broadcast_to(mine[None], (16, UNIT, WIDE)), ("y_hi", "z")).reshape(16 * UNIT, WIDE)
    group, first = lax.optimization_barrier((group, first))
    got = lax.all_gather(group, ("x", "core"), axis=0, tiled=True)
    taper = taper_call(batch_order, first, vert_weight, horiz, obs_cell, obs_level)
    post_pert, post_mean = filter_call(where, batch_order, first, vert_weight, horiz, got, pert, mean, taper)
    return post_mean.reshape(prior_mean.shape), post_pert.reshape(prior_pert.shape)


def solution(mesh):
    whole = Mesh(mesh.devices.reshape(2, 4, 8, 2, NLEV), AXES + ("y_lo",))
    return jax.shard_map(
        shards,
        mesh=whole,
        in_specs=(
            P("y_lo", AXES),
            P(None, "y_lo", AXES),
            P(),
            P(),
            P(),
            P(),
            P(),
            P(),
            P(),
            P(),
        ),
        out_specs=(P("y_lo", AXES), P(None, "y_lo", AXES)),
        check_vma=False,
    )
```

time: 213 us -> 165 us (0.77)
  the two profiles are of different devices: /device:TPU:1 before, /device:TPU:22 now
where the time goes in v4:
time: 165 us; the launch traced here: 164 us
  Pallas kernels  92.4 us (56%)
  blocking collectives  47.4 us (29%)
  between operations  14.2 us (9%)
  local copies, waits for them, and re-layouts  9.3 us (6%)
    all_to_all x2, blocking collectives, exchange(): return lax.all_to_all(block, axes, 0, 0)  47.4 us
    pallas_call x1, Pallas kernels, filter_call(): pl.pallas_call(filter_kernel, out_shape=(jax.ShapeDtypeStruct((MEMBERS, C...  47.3 us
    pallas_call x1, Pallas kernels, taper_call(): pl.pallas_call(taper_kernel, out_shape=jax.ShapeDtypeStruct((NTILES, TILE...  41.6 us
    unnamed x26, local copies, waits for them, and re-layouts  8.56 us
    pallas_call x1, Pallas kernels, select_call(): pl.pallas_call(select_kernel, out_shape=(jax.ShapeDtypeStruct((NLEV, UNIT...  3.43 us
  transfers between devices with their start and end apart: 1, of which 0 were waited for; matrix products, arithmetic and copies ran while one was open for 0% of the time, Pallas kernels for 25%

profile of v4, /device:TPU:22, one launch (start us, length us, event | category | flops | bytes accessed | tf_op | source)
XLA Modules:
  0.0 163.9 jit_solution(12309436450518731390)
XLA Ops:
  7.2 0.0 all-gather.2.cloned.1.call-start
  7.2 1.6 copy.15
  8.8 0.6 pad_add_fusion.where_ref
  9.5 0.0 copy-start.11
  9.5 3.4 %shard_map.113 = (bf16[4,144,128]{2,1,0:T(8,128)(2,1)}, s32[8,128]{1,0:T(8,128)}) custom-call(s32[2]{0:T(128)} %pad_add_fusion.where_ref, s32[8]{0:T(128)} %order_ref.3, s32[8,128]{1,0:T(8,128)} %count_hbm.1, s32[8,3072]{1,0:T(8,128)} %cell_ref.1, s32[8,3072]{1,0:T(8,128)} %lev_ref.1, f32[8,3072]{1,0:T(8,128)} %value_hbm.1, f32[8,3072]{1,0:T(8,128)} %var_hbm.1, ...), custom_call_target="tpu_custom_call" | custom-call | tf_op jit(solution)/shard_map/pallas_call | solution.py:364
  12.9 9.6 %all_to_all.10 = bf16[4,144,128]{2,1,0:T(8,128)(2,1)S(1)} all-to-all(bf16[4,144,128]{2,1,0:T(8,128)(2,1)} %get-tuple-element.8), channel_id=1, replica_groups=mesh['y_hi'=2,'x'=4,'z'=8,'core'=2,'y_lo'=4] {'y_lo'}, dimensions={0} | all-to-all | bytes 294912 | tf_op jit(solution)/shard_map/all_to_all | solution.py:432
  22.5 0.1 broadcast_in_dim.4
  22.6 37.8 %all_to_all.11 = bf16[16,144,128]{2,1,0:T(8,128)(2,1)} all-to-all(bf16[16,144,128]{2,1,0:T(8,128)(2,1)S(1)} %broadcast_in_dim.4), channel_id=1, replica_groups=mesh['y_hi'=2,'x'=4,'z'=8,'core'=2,'y_lo'=4] {'y_hi','z'}, dimensions={0} | all-to-all | bytes 1179648 | tf_op jit(solution)/shard_map/all_to_all | solution.py:432
  60.4 0.0 all-gather.2.cloned.1.call-update
  60.4 0.7 pad.4.horiz_ref
  61.1 0.9 copy-done.2
  62.0 0.9 copy-done.3
  62.9 0.7 copy-done.5
  63.5 0.7 copy-done.7
  64.2 0.7 copy-done.10
  64.9 41.6 %shard_map.114.taper_hbm = bf16[30,512,1024]{2,1,0:T(8,128)(2,1)} custom-call(s32[8]{0:T(128)S(1)} %copy-done.7, s32[8,128]{1,0:T(8,128)S(1)} %copy-done.5, f32[4]{0:T(128)S(1)} %copy-done.10, f32[1,128]{1,0:T(1,128)S(1)} %pad.4.horiz_ref, s32[8,3072]{1,0:T(8,128)S(1)} %copy-done.2, s32[8,3072]{1,0:T(8,128)S(1)} %copy-done.3), custom_call_target="tpu_custom_call" | custom-call | flops 16106127360 | bytes 33554432 | tf_op jit(solution)/shard_map/pallas_call | solution.py:390
  106.5 0.0 all-gather.2.cloned.1.call-done.got_ref
  106.5 0.0 copy-done.1
  106.5 0.0 copy-done.4
  106.6 0.0 copy-done.8
  106.6 0.0 copy-done.9
  106.6 2.3 %copy-done = bf16[18432,128]{1,0:T(8,128)(2,1)S(1)} copy-done((bf16[18432,128]{1,0:T(8,128)(2,1)S(1)}, bf16[18432,128]{1,0:T(8,128)(2,1)}, u32[]{:S(2)}) %copy-start) | copy-done | bytes 4718616
  108.9 47.3 %shard_map.115 = (f32[80,512]{1,0:T(8,128)S(1)}, f32[1,512]{1,0:T(1,128)}) custom-call(s32[2]{0:T(128)S(1)} %copy-done.9, s32[8]{0:T(128)S(1)} %copy-done.8, s32[8,128]{1,0:T(8,128)S(1)} %copy-done.6, f32[4]{0:T(128)S(1)} %copy-done.11, f32[1,128]{1,0:T(1,128)S(1)} %pad.4.horiz_ref, bf16[18432,128]{1,0:T(8,128)(2,1)S(1)} %copy-done, f32[80,512]{1,0:T(8,128)S(1)} %bitcast.9, ...), custom_call_target="tpu_custom_call" | custom-call | tf_op jit(solution)/shard_map/pallas_call | solution.py:412
  156.2 0.8 copy.12
  (14 shorter events, 0.0 us)
Async XLA Ops:
  7.2 99.4 %all-gather.2.cloned.1.call-start = ((), (), s32[]{:S(2)}) async-start(), calls=%async_computation.2 | async-start | bytes 5308416 | tf_op jit(solution)/shard_map/all_gather | solution.py:458
  9.5 97.1 %copy-start.1 = (f32[80,1,512]{2,0,1:T(8,128)S(1)}, f32[80,1,512]{2,0,1:T(8,128)}, u32[]{:S(2)}) copy-start(f32[80,1,512]{2,0,1:T(8,128)} %copy.15) | copy-start | bytes 491524
  9.5 97.1 %copy-start.4 = (f32[1,512]{1,0:T(1,128)S(1)}, f32[1,512]{1,0:T(1,128)}, u32[]{:S(2)}) copy-start(f32[1,512]{1,0:T(1,128)} %mean_ref.1) | copy-start | bytes 6148
  9.5 97.1 %copy-start.8 = (s32[8]{0:T(128)S(1)}, s32[8]{0:T(128)}, u32[]{:S(2)}) copy-start(s32[8]{0:T(128)} %order_ref.3) | copy-start | bytes 100
  9.5 97.1 %copy-start.9 = (s32[2]{0:T(128)S(1)}, s32[2]{0:T(128)}, u32[]{:S(2)}) copy-start(s32[2]{0:T(128)} %pad_add_fusion.where_ref) | copy-start | bytes 28
  9.5 97.1 %copy-start.11 = (f32[4]{0:T(128)S(1)}, f32[4]{0:T(128)}, u32[]{:S(2)}) copy-start(f32[4]{0:T(128)} %vert_ref.3) | copy-start | bytes 52
  12.9 93.7 %copy-start.6 = (s32[8,128]{1,0:T(8,128)S(1)}, s32[8,128]{1,0:T(8,128)}, u32[]{:S(2)}) copy-start(s32[8,128]{1,0:T(8,128)} %get-tuple-element.10.first_ref) | copy-start | bytes 12292
  61.1 0.9 copy-start.2
  62.0 0.9 copy-start.3
  62.9 0.7 copy-start.5
  63.5 0.7 copy-start.7
  64.2 0.7 copy-start.10
  106.6 2.3 %copy-start = (bf16[18432,128]{1,0:T(8,128)(2,1)S(1)}, bf16[18432,128]{1,0:T(8,128)(2,1)}, u32[]{:S(2)}) copy-start(bf16[18432,128]{1,0:T(8,128)(2,1)} %all-gather.2.cloned.1.call-done.got_ref) | copy-start | bytes 14155780
Sparse Core Ops, SparseCore 0:
  60.5 31.1 all-gather.1

commit v5 on v4

--- a/solution.py
+++ b/solution.py
@@ -14,6 +14,7 @@
 NPATCH = 128
 NLEV = 4
 BIN = 16
+NBIN = 16
 CAP = 24
 NOBS = 1024
 CELLS = TX * TY
@@ -22,7 +23,9 @@
 TILE = 512
 SPAN = 256
 LIVE_COLS = NBATCH * NOBS
-COLS = LIVE_COLS + CELLS
+SLAB = NOBS + 32
+OWN = NBATCH * SLAB
+PARTS = 4
 NTILES = NBATCH * (NBATCH - 1) // 2 * (NOBS // TILE)
 INNOV, VAR, POS_X, POS_Y, POS_Z = 80, 83, 86, 87, 88
 VMEM = pltpu.VMEM
@@ -35,6 +38,22 @@
     high = value.astype(BF16).astype(F32)
     mid = (value - high).astype(BF16).astype(F32)
     return high, mid, value - high - mid
+
+
+def fetch(pairs, sems):
+    copies = [pltpu.make_async_copy(one, other, sems.at[i]) for i, (one, other) in enumerate(pairs)]
+    for copy in copies:
+        copy.start()
+    for copy in copies:
+        copy.wait()
+
+
+def horizontal(horiz_ref):
+    lane = lax.broadcasted_iota(jnp.int32, (1, WIDE), 1)
+    table = jnp.zeros((1, WIDE), F32)
+    for step in range(NBIN):
+        table = jnp.where(lane == step, horiz_ref[step], table)
+    return table
 
 
 def select_kernel(
@@ -46,7 +65,7 @@
     value_hbm,
     var_hbm,
     mean_hbm,
-    pert_ref,
+    pert_hbm,
     out_ref,
     first_ref,
     order_ref,
@@ -57,6 +76,7 @@
     value_ref,
     var_ref,
     mean_ref,
+    pert_ref,
     sems,
 ):
     patch = where_ref[0]
@@ -74,12 +94,9 @@
         (value_hbm.at[:, near], value_ref),
         (var_hbm.at[:, near], var_ref),
         (mean_hbm, mean_ref),
+        (pert_hbm.at[:, 0, :], pert_ref),
     ]
-    copies = [pltpu.make_async_copy(one, other, sems.at[i]) for i, (one, other) in enumerate(pairs)]
-    for copy in copies:
-        copy.start()
-    for copy in copies:
-        copy.wait()
+    fetch(pairs, sems)
 
     def column(ref):
         rows = pltpu.roll(ref[...].astype(F32), shift, 1)[:, :WIDE]
@@ -116,17 +133,15 @@
     for at, item in enumerate([*split3(innov), *split3(var), obs_x, obs_y, lev]):
         out = jnp.where(lane == INNOV + at, item, out)
     out = jnp.where(own, out, 0.0).astype(BF16)
-    for z in range(NLEV):
-        out_ref[z] = out
+    for other in range(2 * NLEV):
+        out_ref[other] = out
 
 
 def gathered(patch):
-    return (((patch >> 4) & 3) * 2 + (patch & 1)) * 16 + (patch >> 6) * 8 + ((patch >> 1) & 7)
-
-
-def spots(g):
-    x, core, y_hi = g // 4, g // 2 % 2, g % 2
-    return y_hi * 64 + x * 16 + core, g * 8
+    return (patch & 15) * 8 + ((patch >> 4) & 3) * 2 + (patch >> 6)
+
+
+GROUP = [(i >> 1) * 16 + (i & 1) * 64 for i in range(8)]
 
 
 def first_tile(k):
@@ -134,8 +149,43 @@
 
 
 def taper_kernel(
-    order_ref, first_ref, vert_ref, horiz_ref, cell_ref, lev_ref, out_hbm, code_ref, slots, place, dist, tab_x, tab_y, levw, bufs, sems
+    order_hbm,
+    first_hbm,
+    vert_hbm,
+    horiz_hbm,
+    cell_hbm,
+    lev_hbm,
+    out_hbm,
+    order_ref,
+    first_ref,
+    vert_ref,
+    horiz_ref,
+    cell_ref,
+    lev_ref,
+    code_ref,
+    slots,
+    place,
+    hot_x,
+    hot_y,
+    dist,
+    tab_x,
+    tab_y,
+    levw,
+    bufs,
+    fetched,
+    sems,
 ):
+    fetch(
+        [
+            (order_hbm, order_ref),
+            (first_hbm, first_ref),
+            (vert_hbm, vert_ref),
+            (horiz_hbm, horiz_ref),
+            (cell_hbm, cell_ref),
+            (lev_hbm, lev_ref),
+        ],
+        fetched,
+    )
     spot = lax.broadcasted_iota(jnp.int32, (8, NPATCH * CAP), 1).astype(F32)
     patch = ((spot + 0.5) * (1.0 / CAP)).astype(jnp.int32)
     cell = cell_ref[...]
@@ -151,9 +201,8 @@
         pick = order_ref[k]
 
         def put(g, unused):
-            patch0, row0 = spots(g)
-            for z in range(8):
-                p = patch0 + 2 * z
+            for step in GROUP:
+                p = g + step
                 rows = slots[pl.ds(pl.multiple_of(p * CAP, 8), CAP), :]
                 place[pl.ds(k * NOBS + first_ref[pick, p], CAP), :] = rows
             return unused
@@ -162,8 +211,15 @@
 
     lax.fori_loop(0, NBATCH, compact, 0)
 
+    def mark(t, unused):
+        here = pl.ds(pl.multiple_of(t * TILE, TILE), TILE)
+        codes = place[here, :].astype(jnp.int32)
+        hot_x[here, :] = hot(codes >> 10, TILE)
+        hot_y[here, :] = hot((codes >> 2) & 255, TILE)
+        return unused
+
     def lookup(bins):
-        table = jnp.broadcast_to(horiz_ref[...], (bins.shape[0], WIDE))
+        table = jnp.broadcast_to(horizontal(horiz_ref), (bins.shape[0], WIDE))
         parts = [
             jnp.take_along_axis(table, bins[:, j : j + WIDE], axis=1) for j in range(0, bins.shape[1], WIDE)
         ]
@@ -183,20 +239,19 @@
         parts = [jnp.where(index - j == lane, 1.0, 0.0).astype(BF16) for j in range(0, SPAN, WIDE)]
         return jnp.concatenate(parts, axis=1)
 
+    lax.fori_loop(0, LIVE_COLS // TILE, mark, 0)
+
     def out_copy(n):
         return pltpu.make_async_copy(bufs.at[n % 2], out_hbm.at[n], sems.at[n % 2])
 
     def batch(k, n):
-        codes = place[pl.ds(pl.multiple_of(k * NOBS, NOBS), NOBS), :].astype(jnp.int32)
-        obs_z = codes.astype(F32).T[:1].astype(jnp.int32) & 3
+        rows = pl.ds(pl.multiple_of(k * NOBS, NOBS), NOBS)
+        obs_z = place[rows, :].T[:1].astype(jnp.int32) & 3
         lane = lax.broadcasted_iota(jnp.int32, (1, NOBS), 1)
         vary = 1.0 + (lane & 63).astype(F32) * (1.0 / 64.0)
         contract = (((1,), (1,)), ((), ()))
-        for tab, index, at, factor in (
-            (tab_x, codes >> 10, 0, vary),
-            (tab_y, (codes >> 2) & 255, 2, 1.0 / vary),
-        ):
-            here = hot(index, NOBS)
+        for tab, hot_rows, at, factor in ((tab_x, hot_x, 0, vary), (tab_y, hot_y, 2, 1.0 / vary)):
+            here = hot_rows[rows, :]
             full = lax.dot_general(dist[at], here, contract, preferred_element_type=F32)
             full = full + lax.dot_general(dist[at + 1], here, contract, preferred_element_type=F32)
             tab[...] = (full * factor).astype(BF16)
@@ -208,10 +263,10 @@
             levw[z : z + 1, :] = found
 
         def tile(t, n):
-            codes = place[pl.ds(pl.multiple_of(t * TILE, TILE), TILE), :].astype(jnp.int32)
-            lhs_x = hot(codes >> 10, TILE)
-            lhs_y = hot((codes >> 2) & 255, TILE)
-            cell_z = codes & 3
+            here = pl.ds(pl.multiple_of(t * TILE, TILE), TILE)
+            lhs_x = hot_x[here, :]
+            lhs_y = hot_y[here, :]
+            cell_z = place[here, :].astype(jnp.int32) & 3
             cell_z = jnp.concatenate([cell_z, cell_z], axis=1)
 
             @pl.when(n >= 2)
@@ -238,6 +293,16 @@
 
 def filter_kernel(
     where_ref,
+    order_hbm,
+    first_hbm,
+    vert_hbm,
+    horiz_hbm,
+    got_hbm,
+    pert_hbm,
+    mean_hbm,
+    taper_hbm,
+    post_pert_hbm,
+    post_mean_ref,
     order_ref,
     first_ref,
     vert_ref,
@@ -245,11 +310,10 @@
     got_ref,
     pert_ref,
     mean_ref,
-    taper_hbm,
-    post_pert_ref,
-    post_mean_ref,
     state,
     bufs,
+    fetched,
+    arrived,
     sems,
 ):
     patch = where_ref[0]
@@ -258,28 +322,45 @@
     def taper_copy(n):
         return pltpu.make_async_copy(taper_hbm.at[n], bufs.at[n % 2], sems.at[n % 2])
 
+    def part_copy(c):
+        rows = pl.ds(c * (NPATCH * UNIT // PARTS), NPATCH * UNIT // PARTS)
+        return pltpu.make_async_copy(got_hbm.at[rows, :], got_ref.at[rows, :], arrived.at[c])
+
+    for c in range(PARTS):
+        part_copy(c).start()
+    fetch(
+        [
+            (order_hbm, order_ref),
+            (first_hbm, first_ref),
+            (vert_hbm, vert_ref),
+            (horiz_hbm, horiz_ref),
+            (pert_hbm.at[:, 0, :], pert_ref),
+            (mean_hbm, mean_ref),
+        ],
+        fetched,
+    )
     taper_copy(0).start()
-
-    for k in range(NBATCH):
-        skip = (k % 2) * 8
-        pick = order_ref[k]
-
-        def place(g, unused, k=k, skip=skip, pick=pick):
-            patch0, row0 = spots(g)
-            for z in range(8):
-                at = pl.multiple_of(row0 * UNIT + (z * UNIT + k * CAP - skip), 16)
-                rows = got_ref[pl.ds(at, 32), :].astype(F32)
-                state[pl.ds(k * NOBS + first_ref[pick, patch0 + 2 * z], CAP), :] = rows[skip : skip + CAP]
-            return unused
-
-        lax.fori_loop(0, NPATCH // 8, place, 0)
     own = jnp.concatenate(
         [pert_ref[...], -mean_ref[...], jnp.zeros((WIDE - 81, CELLS), F32)], axis=0
     )
-    state[LIVE_COLS:COLS, :] = own.T
+    state[OWN : OWN + CELLS, :] = own.T
+
+    def place(g, unused):
+        for i, step in enumerate(GROUP):
+            for k in range(NBATCH):
+                skip = (k % 2) * 8
+                at = pl.multiple_of(g * (8 * UNIT) + (i * UNIT + k * CAP - skip), 16)
+                rows = got_ref[pl.ds(at, 32), :].astype(F32)
+                first = first_ref[order_ref[k], g + step]
+                state[pl.ds(k * SLAB + first, CAP), :] = rows[skip : skip + CAP]
+        return unused
+
+    for c in range(PARTS):
+        part_copy(c).wait()
+        lax.fori_loop(c * (16 // PARTS), (c + 1) * (16 // PARTS), place, 0)
 
     def lookup(bins):
-        table = jnp.broadcast_to(horiz_ref[...], (bins.shape[0], WIDE))
+        table = jnp.broadcast_to(horizontal(horiz_ref), (bins.shape[0], WIDE))
         parts = [
             jnp.take_along_axis(table, bins[:, j : j + WIDE], axis=1) for j in range(0, bins.shape[1], WIDE)
         ]
@@ -299,7 +380,7 @@
         return found
 
     def batch(k, n):
-        start = pl.multiple_of(k * NOBS, NOBS)
+        start = pl.multiple_of(k * SLAB, 32)
         block = state[pl.ds(start, NOBS), :].T
         innov = block[INNOV : INNOV + 1] + block[INNOV + 1 : INNOV + 2] + block[INNOV + 2 : INNOV + 3]
         obs_var = block[VAR : VAR + 1] + block[VAR + 1 : VAR + 2] + block[VAR + 2 : VAR + 3]
@@ -316,7 +397,7 @@
         own_e = lax.broadcasted_iota(jnp.int32, (TY, NOBS), 0) + patch % PROWS * TY
         weight_x = lookup(bins_x(own_a.astype(F32), obs_x)) * (vertical(jnp.abs(obs_z - level)) * scale)
         weight_y = lookup(bins_y(own_e.astype(F32), obs_y))
-        cells = state[LIVE_COLS:COLS, :]
+        cells = state[OWN : OWN + CELLS, :]
         lhs = cells.astype(BF16)
         change = jnp.zeros((CELLS, WIDE), F32)
         for j in range(0, NOBS, SPAN):
@@ -330,7 +411,7 @@
                 axis=0,
             )
             change = change + jnp.dot(gain, coeffs[part], preferred_element_type=F32)
-        state[LIVE_COLS:COLS, :] = cells - change
+        state[OWN : OWN + CELLS, :] = cells - change
 
         def tile(t, n):
             taper_copy(n).wait()
@@ -339,7 +420,7 @@
             def _():
                 taper_copy(n + 1).start()
 
-            at = pl.multiple_of(t * TILE, TILE)
+            at = pl.multiple_of((t >> 1) * SLAB + (t & 1) * TILE, 32)
             cells = state[pl.ds(at, TILE), :]
             lhs = cells.astype(BF16)
             taper = bufs.at[n % 2]
@@ -355,22 +436,30 @@
         return lax.fori_loop(first_tile(k), LIVE_COLS // TILE, tile, n)
 
     lax.fori_loop(0, NBATCH, batch, 0)
-    block = state[LIVE_COLS:COLS, :].T
-    post_pert_ref[...] = block[:MEMBERS]
+    block = state[OWN : OWN + CELLS, :].T
+    pert_ref[...] = block[:MEMBERS]
     post_mean_ref[...] = -block[MEMBERS : MEMBERS + 1]
+    fetch([(pert_ref, post_pert_hbm.at[:, 0, :])], fetched)
+
+
+HBM = pltpu.HBM
+DMA = pltpu.SemaphoreType.DMA
+GRANT = pltpu.CompilerParams(vmem_limit_bytes=60 << 20)
+
+
+def spec(space):
+    return pl.BlockSpec(memory_space=space)
 
 
 def select_call(where, order, count, cell, lev, value, var, mean, pert):
     return pl.pallas_call(
         select_kernel,
         out_shape=(
-            jax.ShapeDtypeStruct((NLEV, UNIT, WIDE), BF16),
+            jax.ShapeDtypeStruct((2 * NLEV, UNIT, WIDE), BF16),
             jax.ShapeDtypeStruct((8, NPATCH), jnp.int32),
         ),
-        in_specs=[pl.BlockSpec(memory_space=SMEM)]
-        + [pl.BlockSpec(memory_space=pltpu.HBM)] * 7
-        + [pl.BlockSpec(memory_space=VMEM)],
-        out_specs=(pl.BlockSpec(memory_space=VMEM),) * 2,
+        in_specs=[spec(SMEM)] + [spec(HBM)] * 8,
+        out_specs=(spec(VMEM),) * 2,
         scratch_shapes=[
             SMEM((8,), jnp.int32),
             SMEM((8, NPATCH), jnp.int32),
@@ -380,9 +469,10 @@
             VMEM((8, 2 * WIDE), F32),
             VMEM((8, 2 * WIDE), F32),
             VMEM((1, CELLS), F32),
-            pltpu.SemaphoreType.DMA((8,)),
+            VMEM((MEMBERS, CELLS), F32),
+            DMA((9,)),
         ],
-        compiler_params=pltpu.CompilerParams(vmem_limit_bytes=60 << 20),
+        compiler_params=GRANT,
     )(where, order, count, cell, lev, value, var, mean, pert)
 
 
@@ -390,20 +480,29 @@
     return pl.pallas_call(
         taper_kernel,
         out_shape=jax.ShapeDtypeStruct((NTILES, TILE, NOBS), BF16),
-        in_specs=[pl.BlockSpec(memory_space=SMEM)] * 3 + [pl.BlockSpec(memory_space=VMEM)] * 3,
-        out_specs=pl.BlockSpec(memory_space=pltpu.HBM),
+        in_specs=[spec(HBM)] * 6,
+        out_specs=spec(HBM),
         scratch_shapes=[
+            SMEM((8,), jnp.int32),
+            SMEM((8, NPATCH), jnp.int32),
+            SMEM((NLEV,), F32),
+            SMEM((NBIN,), F32),
+            VMEM((8, NPATCH * CAP), jnp.int32),
+            VMEM((8, NPATCH * CAP), jnp.int32),
             VMEM((8, NPATCH * CAP), F32),
             VMEM((NPATCH * CAP, WIDE), F32),
             VMEM((LIVE_COLS + 2 * CAP, WIDE), F32),
+            VMEM((LIVE_COLS, SPAN), BF16),
+            VMEM((LIVE_COLS, SPAN), BF16),
             VMEM((4, SPAN, SPAN), BF16),
             VMEM((SPAN, NOBS), BF16),
             VMEM((SPAN, NOBS), BF16),
             VMEM((8, NOBS), F32),
             VMEM((2, TILE, NOBS), BF16),
-            pltpu.SemaphoreType.DMA((2,)),
+            DMA((6,)),
+            DMA((2,)),
         ],
-        compiler_params=pltpu.CompilerParams(vmem_limit_bytes=48 << 20),
+        compiler_params=GRANT,
         cost_estimate=pl.CostEstimate(flops=2 * 15 * NOBS * NOBS * 512, bytes_accessed=32 << 20, transcendentals=0),
     )(order, first, vert, horiz, cell, lev)
 
@@ -412,19 +511,26 @@
     return pl.pallas_call(
         filter_kernel,
         out_shape=(
-            jax.ShapeDtypeStruct((MEMBERS, CELLS), F32),
+            jax.ShapeDtypeStruct((MEMBERS, 1, CELLS), F32),
             jax.ShapeDtypeStruct((1, CELLS), F32),
         ),
-        in_specs=[pl.BlockSpec(memory_space=SMEM)] * 4
-        + [pl.BlockSpec(memory_space=VMEM)] * 4
-        + [pl.BlockSpec(memory_space=pltpu.HBM)],
-        out_specs=(pl.BlockSpec(memory_space=VMEM),) * 2,
+        in_specs=[spec(SMEM)] + [spec(HBM)] * 8,
+        out_specs=(spec(HBM), spec(VMEM)),
         scratch_shapes=[
-            VMEM((COLS, WIDE), F32),
+            SMEM((8,), jnp.int32),
+            SMEM((8, NPATCH), jnp.int32),
+            SMEM((NLEV,), F32),
+            SMEM((NBIN,), F32),
+            VMEM((NPATCH * UNIT, WIDE), BF16),
+            VMEM((MEMBERS, CELLS), F32),
+            VMEM((1, CELLS), F32),
+            VMEM((OWN + CELLS, WIDE), F32),
             VMEM((2, TILE, NOBS), BF16),
-            pltpu.SemaphoreType.DMA((2,)),
+            DMA((6,)),
+            DMA((PARTS,)),
+            DMA((2,)),
         ],
-        compiler_params=pltpu.CompilerParams(vmem_limit_bytes=48 << 20),
+        compiler_params=GRANT,
     )(where, order, first, vert, horiz, got, pert, mean, taper)
 
 
@@ -448,17 +554,20 @@
     vert_weight,
 ):
     where = jnp.stack([lax.axis_index(AXES), lax.axis_index("y_lo")]).astype(jnp.int32)
-    pert = prior_pert.reshape(MEMBERS, CELLS)
-    mean = prior_mean.reshape(1, CELLS)
-    mine, first = select_call(where, batch_order, obs_count, obs_cell, obs_level, obs_value, obs_var, mean, pert)
-    horiz = jnp.pad(horiz_weight[None, :], ((0, 0), (0, WIDE - horiz_weight.shape[0])))
-    mine = jnp.sum(exchange(mine, "y_lo").astype(F32), axis=0).astype(BF16)
-    group = exchange(jnp.broadcast_to(mine[None], (16, UNIT, WIDE)), ("y_hi", "z")).reshape(16 * UNIT, WIDE)
+    mean = prior_mean
+    mine, first = select_call(
+        where, batch_order, obs_count, obs_cell, obs_level, obs_value, obs_var, mean, prior_pert
+    )
+    ring = exchange(mine, ("y_hi", "y_lo")).reshape(2, NLEV, UNIT, WIDE)
+    pair = jnp.sum(ring.astype(F32), axis=1).astype(BF16).reshape(1, 2 * UNIT, WIDE)
+    group = exchange(jnp.broadcast_to(pair, (4, 2 * UNIT, WIDE)), "x").reshape(8 * UNIT, WIDE)
     group, first = lax.optimization_barrier((group, first))
-    got = lax.all_gather(group, ("x", "core"), axis=0, tiled=True)
-    taper = taper_call(batch_order, first, vert_weight, horiz, obs_cell, obs_level)
-    post_pert, post_mean = filter_call(where, batch_order, first, vert_weight, horiz, got, pert, mean, taper)
-    return post_mean.reshape(prior_mean.shape), post_pert.reshape(prior_pert.shape)
+    got = lax.all_gather(group, ("z", "core"), axis=0, tiled=True)
+    taper = taper_call(batch_order, first, vert_weight, horiz_weight, obs_cell, obs_level)
+    post_pert, post_mean = filter_call(
+        where, batch_order, first, vert_weight, horiz_weight, got, prior_pert, mean, taper
+    )
+    return post_mean, post_pert
 
 
 def solution(mesh):

time: 165 us -> 144 us (0.87)
  the two profiles are of different devices: /device:TPU:22 before, /device:TPU:1 now
where the time goes in v5:
time: 144 us; the launch traced here: 143 us
  Pallas kernels  92 us (64%)
  blocking collectives  28.1 us (20%)
  between operations  14.1 us (10%)
  waiting for transfers between devices  7.99 us (6%)
    pallas_call x1, Pallas kernels, filter_call(): pl.pallas_call(filter_kernel, out_shape=(jax.ShapeDtypeStruct((MEMBERS, 1...  48.9 us
    pallas_call x1, Pallas kernels, taper_call(): pl.pallas_call(taper_kernel, out_shape=jax.ShapeDtypeStruct((NTILES, TILE...  39.7 us
    all_to_all x2, blocking collectives, exchange(): return lax.all_to_all(block, axes, 0, 0)  28.1 us
    all_gather x1, waiting for transfers between devices, shards(): got = lax.all_gather(group, ('z', 'core'), axis=0, tiled=True)  7.97 us
    pallas_call x1, Pallas kernels, select_call(): pl.pallas_call(select_kernel, out_shape=(jax.ShapeDtypeStruct((2 * NLEV,...  3.42 us
  transfers between devices with their start and end apart: 1, of which 1 were waited for; matrix products, arithmetic and copies ran while one was open for 0% of the time, Pallas kernels for 28%

profile of v5, /device:TPU:1, one launch (start us, length us, event | category | flops | bytes accessed | tf_op | source)
XLA Modules:
  0.0 142.9 jit_solution(59577293180929947)
XLA Ops:
  7.2 0.0 all-gather.2.cloned.1.call-start
  7.2 0.6 pad_add_fusion.where_ref
  7.9 3.4 %shard_map.113 = (bf16[8,144,128]{2,1,0:T(8,128)(2,1)}, s32[8,128]{1,0:T(8,128)}) custom-call(s32[2]{0:T(128)} %pad_add_fusion.where_ref, s32[8]{0:T(128)} %order_hbm.5, s32[8,128]{1,0:T(8,128)} %count_hbm.1, s32[8,3072]{1,0:T(8,128)} %cell_hbm.3, s32[8,3072]{1,0:T(8,128)} %lev_hbm.3, f32[8,3072]{1,0:T(8,128)} %value_hbm.1, f32[8,3072]{1,0:T(8,128)} %var_hbm.1, ...), custom_call_target="tpu_custom_call" | custom-call | tf_op jit(solution)/shard_map/pallas_call | solution.py:455
  11.3 17.4 %all_to_all.10 = bf16[8,144,128]{2,1,0:T(8,128)(2,1)S(1)} all-to-all(bf16[8,144,128]{2,1,0:T(8,128)(2,1)} %get-tuple-element.8), channel_id=1, replica_groups=mesh['y_hi'=2,'x'=4,'z'=8,'core'=2,'y_lo'=4] {'y_hi','y_lo'}, dimensions={0} | all-to-all | bytes 589824 | tf_op jit(solution)/shard_map/all_to_all | solution.py:538
  28.7 10.8 %all_to_all.11 = bf16[4,288,128]{2,1,0:T(8,128)(2,1)} all-to-all(bf16[4,288,128]{2,1,0:T(8,128)(2,1)S(1)} %broadcast_in_dim.8), channel_id=1, replica_groups=mesh['y_hi'=2,'x'=4,'z'=8,'core'=2,'y_lo'=4] {'x'}, dimensions={0} | all-to-all | bytes 589824 | tf_op jit(solution)/shard_map/all_to_all | solution.py:538
  39.5 0.0 all-gather.2.cloned.1.call-update
  39.5 39.7 %shard_map.114.taper_hbm = bf16[30,512,1024]{2,1,0:T(8,128)(2,1)} custom-call(s32[8]{0:T(128)} %order_hbm.5, s32[8,128]{1,0:T(8,128)} %get-tuple-element.10.first_hbm, f32[4]{0:T(128)} %vert_hbm.3, f32[16]{0:T(128)} %horiz_hbm.3, s32[8,3072]{1,0:T(8,128)} %cell_hbm.3, s32[8,3072]{1,0:T(8,128)} %lev_hbm.3), custom_call_target="tpu_custom_call" | custom-call | flops 16106127360 | bytes 33554432 | tf_op jit(solution)/shard_map/pallas_call | solution.py:480
  79.2 8.0 %all-gather.2.cloned.1.call-done.got_hbm = bf16[18432,128]{1,0:T(8,128)(2,1)} async-done(((bf16[1152,128]{1,0:T(8,128)(2,1)}), bf16[18432,128]{1,0:T(8,128)(2,1)}) %all-gather.2.cloned.1.call-update) | async-done | bytes 4718608 | tf_op jit(solution)/shard_map/all_gather | solution.py:565
  87.2 48.9 %shard_map.115 = (f32[80,1,512]{2,1,0:T(1,128)}, f32[1,512]{1,0:T(1,128)}) custom-call(s32[2]{0:T(128)} %pad_add_fusion.where_ref, s32[8]{0:T(128)} %order_hbm.5, s32[8,128]{1,0:T(8,128)} %get-tuple-element.10.first_hbm, f32[4]{0:T(128)} %vert_hbm.3, f32[16]{0:T(128)} %horiz_hbm.3, bf16[18432,128]{1,0:T(8,128)(2,1)} %all-gather.2.cloned.1.call-done.got_hbm, ...), custom_call_target="tpu_custom_call" | custom-call | tf_op jit(solution)/shard_map/pallas_call | solution.py:511
  (2 shorter events, 0.1 us)
Async XLA Ops:
  7.2 80.0 %all-gather.2.cloned.1.call-start = ((), (), s32[]{:S(2)}) async-start(), calls=%async_computation.2 | async-start | bytes 5013504 | tf_op jit(solution)/shard_map/all_gather | solution.py:565
Sparse Core Ops, SparseCore 0:
  39.6 47.4 all-gather.1

commit v6 on v5

--- a/solution.py
+++ b/solution.py
@@ -20,7 +20,8 @@
 CELLS = TX * TY
 UNIT = NBATCH * CAP
 WIDE = 128
-TILE = 512
+TILE = 1024
+PACK = 112
 SPAN = 256
 LIVE_COLS = NBATCH * NOBS
 SLAB = NOBS + 32
@@ -38,6 +39,25 @@
     high = value.astype(BF16).astype(F32)
     mid = (value - high).astype(BF16).astype(F32)
     return high, mid, value - high - mid
+
+
+def packed(rows):
+    base = jnp.concatenate([rows[:96], rows[120:136]], axis=0)
+    thirds = [pltpu.roll(rows[96:120], 96 - 32 * i, 1) for i in range(3)]
+    thirds += [pltpu.roll(rows[136:144], 96 - 32 * i, 1) for i in range(3)]
+    extra = jnp.concatenate(thirds + [rows[120:136]], axis=0)
+    lane = lax.broadcasted_iota(jnp.int32, base.shape, 1)
+    return jnp.where(lane < 96, base, extra)
+
+
+def unpacked(rows):
+    def joined(start, size):
+        parts = [pltpu.roll(rows[start + i * size : start + (i + 1) * size], 32 * (i + 1), 1) for i in range(3)]
+        lane = lax.broadcasted_iota(jnp.int32, parts[0].shape, 1)
+        return jnp.where(lane < 32, parts[0], jnp.where(lane < 64, parts[1], parts[2]))
+
+    last = jnp.concatenate([rows[96:112], joined(72, 8)], axis=0)
+    return [rows[k * CAP : (k + 1) * CAP] for k in range(4)] + [joined(0, CAP), last]
 
 
 def fetch(pairs, sems):
@@ -132,7 +152,7 @@
     out = jnp.where(lane < MEMBERS, taken, 0.0)
     for at, item in enumerate([*split3(innov), *split3(var), obs_x, obs_y, lev]):
         out = jnp.where(lane == INNOV + at, item, out)
-    out = jnp.where(own, out, 0.0).astype(BF16)
+    out = packed(jnp.where(own, out, 0.0)).astype(BF16)
     for other in range(2 * NLEV):
         out_ref[other] = out
 
@@ -193,11 +213,11 @@
     at_y = (patch % PROWS) * TY + cell % TY
     code_ref[...] = (at_x * 1024 + at_y * NLEV + lev_ref[...]).astype(F32)
 
+    for c in range(NPATCH * CAP // WIDE):
+        part = slice(c * WIDE, (c + 1) * WIDE)
+        slots[part, :] = jnp.concatenate([code_ref[:, part], jnp.zeros((WIDE - 8, WIDE), F32)], axis=0).T
+
     def compact(k, unused):
-        row = code_ref[pl.ds(order_ref[k], 1), :]
-        for c in range(NPATCH * CAP // WIDE):
-            part = slice(c * WIDE, (c + 1) * WIDE)
-            slots[part, :] = jnp.broadcast_to(row[:, part], (WIDE, WIDE)).T
         pick = order_ref[k]
 
         def put(g, unused):
@@ -213,7 +233,12 @@
 
     def mark(t, unused):
         here = pl.ds(pl.multiple_of(t * TILE, TILE), TILE)
-        codes = place[here, :].astype(jnp.int32)
+        rows = place[here, :]
+        lane = lax.broadcasted_iota(jnp.int32, (TILE, WIDE), 1)
+        code = jnp.sum(jnp.where(lane == order_ref[t], rows, 0.0), axis=1, keepdims=True)
+        code = jnp.broadcast_to(code, (TILE, WIDE))
+        place[here, :] = code
+        codes = code.astype(jnp.int32)
         hot_x[here, :] = hot(codes >> 10, TILE)
         hot_y[here, :] = hot((codes >> 2) & 255, TILE)
         return unused
@@ -323,7 +348,7 @@
         return pltpu.make_async_copy(taper_hbm.at[n], bufs.at[n % 2], sems.at[n % 2])
 
     def part_copy(c):
-        rows = pl.ds(c * (NPATCH * UNIT // PARTS), NPATCH * UNIT // PARTS)
+        rows = pl.ds(c * (NPATCH * PACK // PARTS), NPATCH * PACK // PARTS)
         return pltpu.make_async_copy(got_hbm.at[rows, :], got_ref.at[rows, :], arrived.at[c])
 
     for c in range(PARTS):
@@ -347,12 +372,10 @@
 
     def place(g, unused):
         for i, step in enumerate(GROUP):
-            for k in range(NBATCH):
-                skip = (k % 2) * 8
-                at = pl.multiple_of(g * (8 * UNIT) + (i * UNIT + k * CAP - skip), 16)
-                rows = got_ref[pl.ds(at, 32), :].astype(F32)
+            at = pl.multiple_of(g * (8 * PACK) + i * PACK, 16)
+            for k, rows in enumerate(unpacked(got_ref[pl.ds(at, PACK), :].astype(F32))):
                 first = first_ref[order_ref[k], g + step]
-                state[pl.ds(k * SLAB + first, CAP), :] = rows[skip : skip + CAP]
+                state[pl.ds(k * SLAB + first, CAP), :] = rows
         return unused
 
     for c in range(PARTS):
@@ -420,7 +443,7 @@
             def _():
                 taper_copy(n + 1).start()
 
-            at = pl.multiple_of((t >> 1) * SLAB + (t & 1) * TILE, 32)
+            at = pl.multiple_of(t * SLAB, 32)
             cells = state[pl.ds(at, TILE), :]
             lhs = cells.astype(BF16)
             taper = bufs.at[n % 2]
@@ -428,7 +451,7 @@
             for j in range(0, NOBS, SPAN):
                 part = slice(j, j + SPAN)
                 cov = jnp.dot(lhs, prior[:, part], preferred_element_type=F32)
-                gain = (taper[:, part].astype(F32) * (cov * scale[:, part])).astype(BF16)
+                gain = taper[:, part] * (cov * scale[:, part]).astype(BF16)
                 change = change + jnp.dot(gain, coeffs[part], preferred_element_type=F32)
             state[pl.ds(at, TILE), :] = cells - change
             return n + 1
@@ -455,7 +478,7 @@
     return pl.pallas_call(
         select_kernel,
         out_shape=(
-            jax.ShapeDtypeStruct((2 * NLEV, UNIT, WIDE), BF16),
+            jax.ShapeDtypeStruct((2 * NLEV, PACK, WIDE), BF16),
             jax.ShapeDtypeStruct((8, NPATCH), jnp.int32),
         ),
         in_specs=[spec(SMEM)] + [spec(HBM)] * 8,
@@ -521,7 +544,7 @@
             SMEM((8, NPATCH), jnp.int32),
             SMEM((NLEV,), F32),
             SMEM((NBIN,), F32),
-            VMEM((NPATCH * UNIT, WIDE), BF16),
+            VMEM((NPATCH * PACK, WIDE), BF16),
             VMEM((MEMBERS, CELLS), F32),
             VMEM((1, CELLS), F32),
             VMEM((OWN + CELLS, WIDE), F32),
@@ -558,9 +581,9 @@
     mine, first = select_call(
         where, batch_order, obs_count, obs_cell, obs_level, obs_value, obs_var, mean, prior_pert
     )
-    ring = exchange(mine, ("y_hi", "y_lo")).reshape(2, NLEV, UNIT, WIDE)
-    pair = jnp.sum(ring.astype(F32), axis=1).astype(BF16).reshape(1, 2 * UNIT, WIDE)
-    group = exchange(jnp.broadcast_to(pair, (4, 2 * UNIT, WIDE)), "x").reshape(8 * UNIT, WIDE)
+    ring = exchange(mine, ("y_hi", "y_lo")).reshape(2, NLEV, PACK, WIDE)
+    pair = jnp.sum(ring.astype(F32), axis=1).astype(BF16).reshape(1, 2 * PACK, WIDE)
+    group = exchange(jnp.broadcast_to(pair, (4, 2 * PACK, WIDE)), "x").reshape(8 * PACK, WIDE)
     group, first = lax.optimization_barrier((group, first))
     got = lax.all_gather(group, ("z", "core"), axis=0, tiled=True)
     taper = taper_call(batch_order, first, vert_weight, horiz_weight, obs_cell, obs_level)

time: 144 us -> 128 us (0.89)
  Pallas kernels: 92 us -> 74.2 us
  waiting for transfers between devices: 7.99 us -> 11.8 us
    pallas_call x1, Pallas kernels: 48.9 us -> 36.3 us  [filter_call(): pl.pallas_call(filter_kernel, out_shape=(jax.ShapeDtypeStruct((MEMBERS, 1...]
    pallas_call x1, Pallas kernels: 39.7 us -> 34.4 us  [taper_call(): pl.pallas_call(taper_kernel, out_shape=jax.ShapeDtypeStruct((NTILES, TILE...]
    all_gather x1, waiting for transfers between devices: 7.97 us -> 11.7 us  [shards(): got = lax.all_gather(group, ('z', 'core'), axis=0, tiled=True)]
  transfers between devices with their start and end apart: 1 -> 1, of which waited for: 1 -> 1; matrix products, arithmetic and copies ran while one was open for 0% -> 0% of each run, Pallas kernels for 28% -> 27%
where the time goes in v6:
time: 128 us
  Pallas kernels  74.2 us (58%)
  blocking collectives  26.7 us (21%)
  between operations  14.1 us (11%)
  waiting for transfers between devices  11.8 us (9%)
    pallas_call x1, Pallas kernels, filter_call(): pl.pallas_call(filter_kernel, out_shape=(jax.ShapeDtypeStruct((MEMBERS, 1...  36.3 us
    pallas_call x1, Pallas kernels, taper_call(): pl.pallas_call(taper_kernel, out_shape=jax.ShapeDtypeStruct((NTILES, TILE...  34.4 us
    all_to_all x2, blocking collectives, exchange(): return lax.all_to_all(block, axes, 0, 0)  26.7 us
    all_gather x1, waiting for transfers between devices, shards(): got = lax.all_gather(group, ('z', 'core'), axis=0, tiled=True)  11.7 us
    pallas_call x1, Pallas kernels, select_call(): pl.pallas_call(select_kernel, out_shape=(jax.ShapeDtypeStruct((2 * NLEV,...  3.48 us
  transfers between devices with their start and end apart: 1, of which 1 were waited for; matrix products, arithmetic and copies ran while one was open for 0% of the time, Pallas kernels for 27%

profile of v6, /device:TPU:1, one launch (start us, length us, event | category | flops | bytes accessed | tf_op | source)
XLA Modules:
  0.0 127.5 jit_solution(11855154972974699358)
XLA Ops:
  7.2 0.0 all-gather.2.cloned.1.call-start
  7.2 0.7 pad_add_fusion.where_ref
  7.9 3.5 %shard_map.113 = (bf16[8,112,128]{2,1,0:T(8,128)(2,1)}, s32[8,128]{1,0:T(8,128)}) custom-call(s32[2]{0:T(128)} %pad_add_fusion.where_ref, s32[8]{0:T(128)} %order_hbm.5, s32[8,128]{1,0:T(8,128)} %count_hbm.1, s32[8,3072]{1,0:T(8,128)} %cell_hbm.3, s32[8,3072]{1,0:T(8,128)} %lev_hbm.3, f32[8,3072]{1,0:T(8,128)} %value_hbm.1, f32[8,3072]{1,0:T(8,128)} %var_hbm.1, ...), custom_call_target="tpu_custom_call" | custom-call | tf_op jit(solution)/shard_map/pallas_call | solution.py:478
  11.4 16.7 %all_to_all.10 = bf16[8,112,128]{2,1,0:T(8,128)(2,1)S(1)} all-to-all(bf16[8,112,128]{2,1,0:T(8,128)(2,1)} %get-tuple-element.8), channel_id=1, replica_groups=mesh['y_hi'=2,'x'=4,'z'=8,'core'=2,'y_lo'=4] {'y_hi','y_lo'}, dimensions={0} | all-to-all | bytes 458752 | tf_op jit(solution)/shard_map/all_to_all | solution.py:561
  28.1 10.0 %all_to_all.11 = bf16[4,224,128]{2,1,0:T(8,128)(2,1)} all-to-all(bf16[4,224,128]{2,1,0:T(8,128)(2,1)S(1)} %broadcast_in_dim.8), channel_id=1, replica_groups=mesh['y_hi'=2,'x'=4,'z'=8,'core'=2,'y_lo'=4] {'x'}, dimensions={0} | all-to-all | bytes 458752 | tf_op jit(solution)/shard_map/all_to_all | solution.py:561
  38.1 0.0 all-gather.2.cloned.1.call-update
  38.1 34.4 %shard_map.114.taper_hbm = bf16[15,1024,1024]{2,1,0:T(8,128)(2,1)} custom-call(s32[8]{0:T(128)} %order_hbm.5, s32[8,128]{1,0:T(8,128)} %get-tuple-element.10.first_hbm, f32[4]{0:T(128)} %vert_hbm.3, f32[16]{0:T(128)} %horiz_hbm.3, s32[8,3072]{1,0:T(8,128)} %cell_hbm.3, s32[8,3072]{1,0:T(8,128)} %lev_hbm.3), custom_call_target="tpu_custom_call" | custom-call | flops 16106127360 | bytes 33554432 | tf_op jit(solution)/shard_map/pallas_call | solution.py:503
  72.6 11.7 %all-gather.2.cloned.1.call-done.got_hbm = bf16[14336,128]{1,0:T(8,128)(2,1)} async-done(((bf16[896,128]{1,0:T(8,128)(2,1)}), bf16[14336,128]{1,0:T(8,128)(2,1)}) %all-gather.2.cloned.1.call-update) | async-done | bytes 3670032 | tf_op jit(solution)/shard_map/all_gather | solution.py:588
  84.3 36.3 %shard_map.115 = (f32[80,1,512]{2,1,0:T(1,128)}, f32[1,512]{1,0:T(1,128)}) custom-call(s32[2]{0:T(128)} %pad_add_fusion.where_ref, s32[8]{0:T(128)} %order_hbm.5, s32[8,128]{1,0:T(8,128)} %get-tuple-element.10.first_hbm, f32[4]{0:T(128)} %vert_hbm.3, f32[16]{0:T(128)} %horiz_hbm.3, bf16[14336,128]{1,0:T(8,128)(2,1)} %all-gather.2.cloned.1.call-done.got_hbm, ...), custom_call_target="tpu_custom_call" | custom-call | tf_op jit(solution)/shard_map/pallas_call | solution.py:534
  (2 shorter events, 0.1 us)
Async XLA Ops:
  7.2 77.2 %all-gather.2.cloned.1.call-start = ((), (), s32[]{:S(2)}) async-start(), calls=%async_computation.2 | async-start | bytes 3899392 | tf_op jit(solution)/shard_map/all_gather | solution.py:588
Sparse Core Ops, SparseCore 0:
  38.3 46.0 all-gather.1

commit v7 on v6

--- a/solution.py
+++ b/solution.py
@@ -336,6 +336,9 @@
     pert_ref,
     mean_ref,
     state,
+    prior,
+    coeffs,
+    lines,
     bufs,
     fetched,
     arrived,
@@ -402,30 +405,35 @@
             found = jnp.where(apart == float(step), vert_ref[step], found)
         return found
 
-    def batch(k, n):
-        start = pl.multiple_of(k * SLAB, 32)
-        block = state[pl.ds(start, NOBS), :].T
+    def slab(k):
+        return pl.ds(pl.multiple_of(k * SLAB, 32), NOBS)
+
+    def prepare(k, slot):
+        block = state[slab(k), :].T
         innov = block[INNOV : INNOV + 1] + block[INNOV + 1 : INNOV + 2] + block[INNOV + 2 : INNOV + 3]
         obs_var = block[VAR : VAR + 1] + block[VAR + 1 : VAR + 2] + block[VAR + 2 : VAR + 3]
-        obs_x, obs_y, obs_z = block[POS_X : POS_X + 1], block[POS_Y : POS_Y + 1], block[POS_Z : POS_Z + 1]
         row = lax.broadcasted_iota(jnp.int32, (WIDE, NOBS), 0)
-        prior = jnp.where(row < MEMBERS, block, 0.0).astype(BF16)
-        values = prior.astype(F32)
+        rounded = jnp.where(row < MEMBERS, block, 0.0).astype(BF16)
+        values = rounded.astype(F32)
         spread = jnp.sum(values * values, axis=0, keepdims=True) / (MEMBERS - 1.0) + obs_var
         shrink = 1.0 / (1.0 + jnp.sqrt(obs_var / spread))
-        scale = 1.0 / ((MEMBERS - 1.0) * spread)
-        coeffs = jnp.where(row == MEMBERS, innov.astype(BF16).astype(F32), values * shrink).T.astype(BF16)
-
+        prior[slot] = rounded
+        lines[slot, 0:1] = 1.0 / ((MEMBERS - 1.0) * spread)
+        lines[slot, 1:4] = block[POS_X : POS_Z + 1]
+        coeffs[slot] = jnp.where(row == MEMBERS, innov.astype(BF16).astype(F32), values * shrink).T.astype(BF16)
+
+    def own_update(slot, cells):
+        scale, obs_x = lines[slot, 0:1], lines[slot, 1:2]
+        obs_y, obs_z = lines[slot, 2:3], lines[slot, 3:4]
         own_a = lax.broadcasted_iota(jnp.int32, (TX, NOBS), 0) + patch // PROWS * TX
         own_e = lax.broadcasted_iota(jnp.int32, (TY, NOBS), 0) + patch % PROWS * TY
         weight_x = lookup(bins_x(own_a.astype(F32), obs_x)) * (vertical(jnp.abs(obs_z - level)) * scale)
         weight_y = lookup(bins_y(own_e.astype(F32), obs_y))
-        cells = state[OWN : OWN + CELLS, :]
         lhs = cells.astype(BF16)
         change = jnp.zeros((CELLS, WIDE), F32)
         for j in range(0, NOBS, SPAN):
             part = slice(j, j + SPAN)
-            cov = jnp.dot(lhs, prior[:, part], preferred_element_type=F32)
+            cov = jnp.dot(lhs, prior[slot, :, part], preferred_element_type=F32)
             gain = jnp.concatenate(
                 [
                     (cov[a * TY : (a + 1) * TY] * (weight_x[a : a + 1, part] * weight_y[:, part])).astype(BF16)
@@ -433,32 +441,57 @@
                 ],
                 axis=0,
             )
-            change = change + jnp.dot(gain, coeffs[part], preferred_element_type=F32)
-        state[OWN : OWN + CELLS, :] = cells - change
+            change = change + jnp.dot(gain, coeffs[slot, part], preferred_element_type=F32)
+        return cells - change
+
+    def pair_update(slot, cells, n):
+        scale = lines[slot, 0:1]
+        lhs = cells.astype(BF16)
+        taper = bufs.at[n % 2]
+        change = jnp.zeros((TILE, WIDE), F32)
+        for j in range(0, NOBS, SPAN):
+            part = slice(j, j + SPAN)
+            cov = jnp.dot(lhs, prior[slot, :, part], preferred_element_type=F32)
+            gain = taper[:, part] * (cov * scale[:, part]).astype(BF16)
+            change = change + jnp.dot(gain, coeffs[slot, part], preferred_element_type=F32)
+        return cells - change
+
+    def next_taper(n):
+        taper_copy(n).wait()
+
+        @pl.when(n < NTILES - 1)
+        def _():
+            taper_copy(n + 1).start()
+
+    def own_and_first(k, slot, n):
+        next_taper(n)
+        mine, first = state[OWN : OWN + CELLS, :], state[slab(k + 1), :]
+        mine, first = own_update(slot, mine), pair_update(slot, first, n)
+        state[OWN : OWN + CELLS, :] = mine
+        state[slab(k + 1), :] = first
+
+    def batch(k, slot, n):
+        own_and_first(k, slot, n)
+        next_taper(n + 1)
+        cells = state[slab(k + 2), :]
+        prepare(k + 1, 1 - slot)
+        state[slab(k + 2), :] = pair_update(slot, cells, n + 1)
 
         def tile(t, n):
-            taper_copy(n).wait()
-
-            @pl.when(n < NTILES - 1)
-            def _():
-                taper_copy(n + 1).start()
-
-            at = pl.multiple_of(t * SLAB, 32)
-            cells = state[pl.ds(at, TILE), :]
-            lhs = cells.astype(BF16)
-            taper = bufs.at[n % 2]
-            change = jnp.zeros((TILE, WIDE), F32)
-            for j in range(0, NOBS, SPAN):
-                part = slice(j, j + SPAN)
-                cov = jnp.dot(lhs, prior[:, part], preferred_element_type=F32)
-                gain = taper[:, part] * (cov * scale[:, part]).astype(BF16)
-                change = change + jnp.dot(gain, coeffs[part], preferred_element_type=F32)
-            state[pl.ds(at, TILE), :] = cells - change
+            next_taper(n)
+            state[slab(t), :] = pair_update(slot, state[slab(t), :], n)
             return n + 1
 
-        return lax.fori_loop(first_tile(k), LIVE_COLS // TILE, tile, n)
-
-    lax.fori_loop(0, NBATCH, batch, 0)
+        return lax.fori_loop(k + 3, NBATCH, tile, n + 2)
+
+    def two(i, n):
+        return batch(2 * i + 1, 1, batch(2 * i, 0, n))
+
+    prepare(0, 0)
+    total = lax.fori_loop(0, NBATCH // 2 - 1, two, 0)
+    own_and_first(NBATCH - 2, 0, total)
+    prepare(NBATCH - 1, 1)
+    state[OWN : OWN + CELLS, :] = own_update(1, state[OWN : OWN + CELLS, :])
     block = state[OWN : OWN + CELLS, :].T
     pert_ref[...] = block[:MEMBERS]
     post_mean_ref[...] = -block[MEMBERS : MEMBERS + 1]
@@ -548,6 +581,9 @@
             VMEM((MEMBERS, CELLS), F32),
             VMEM((1, CELLS), F32),
             VMEM((OWN + CELLS, WIDE), F32),
+            VMEM((2, WIDE, NOBS), BF16),
+            VMEM((2, NOBS, WIDE), BF16),
+            VMEM((2, 8, NOBS), F32),
             VMEM((2, TILE, NOBS), BF16),
             DMA((6,)),
             DMA((PARTS,)),

time: 128 us -> 127 us (level)
  Pallas kernels: 74.2 us -> 72.8 us
    pallas_call x1, Pallas kernels: 36.3 us -> 34.9 us  [filter_call(): pl.pallas_call(filter_kernel, out_shape=(jax.ShapeDtypeStruct((MEMBERS, 1...]
where the time goes in v7:
time: 127 us; the launch traced here: 126 us
  Pallas kernels  72.8 us (57%)
  blocking collectives  26.7 us (21%)
  between operations  14.1 us (11%)
  waiting for transfers between devices  11.7 us (9%)
    pallas_call x1, Pallas kernels, filter_call(): pl.pallas_call(filter_kernel, out_shape=(jax.ShapeDtypeStruct((MEMBERS, 1...  34.9 us
    pallas_call x1, Pallas kernels, taper_call(): pl.pallas_call(taper_kernel, out_shape=jax.ShapeDtypeStruct((NTILES, TILE...  34.5 us
    all_to_all x2, blocking collectives, exchange(): return lax.all_to_all(block, axes, 0, 0)  26.7 us
    all_gather x1, waiting for transfers between devices, shards(): got = lax.all_gather(group, ('z', 'core'), axis=0, tiled=True)  11.7 us
    pallas_call x1, Pallas kernels, select_call(): pl.pallas_call(select_kernel, out_shape=(jax.ShapeDtypeStruct((2 * NLEV,...  3.49 us
  transfers between devices with their start and end apart: 1, of which 1 were waited for; matrix products, arithmetic and copies ran while one was open for 0% of the time, Pallas kernels for 27%

profile of v7, /device:TPU:1, one launch (start us, length us, event | category | flops | bytes accessed | tf_op | source)
XLA Modules:
  0.0 126.1 jit_solution(2988649908703839176)
XLA Ops:
  7.2 0.0 all-gather.2.cloned.1.call-start
  7.2 0.7 pad_add_fusion.where_ref
  7.9 3.5 %shard_map.113 = (bf16[8,112,128]{2,1,0:T(8,128)(2,1)}, s32[8,128]{1,0:T(8,128)}) custom-call(s32[2]{0:T(128)} %pad_add_fusion.where_ref, s32[8]{0:T(128)} %order_hbm.5, s32[8,128]{1,0:T(8,128)} %count_hbm.1, s32[8,3072]{1,0:T(8,128)} %cell_hbm.3, s32[8,3072]{1,0:T(8,128)} %lev_hbm.3, f32[8,3072]{1,0:T(8,128)} %value_hbm.1, f32[8,3072]{1,0:T(8,128)} %var_hbm.1, ...), custom_call_target="tpu_custom_call" | custom-call | tf_op jit(solution)/shard_map/pallas_call | solution.py:511
  11.4 16.7 %all_to_all.10 = bf16[8,112,128]{2,1,0:T(8,128)(2,1)S(1)} all-to-all(bf16[8,112,128]{2,1,0:T(8,128)(2,1)} %get-tuple-element.8), channel_id=1, replica_groups=mesh['y_hi'=2,'x'=4,'z'=8,'core'=2,'y_lo'=4] {'y_hi','y_lo'}, dimensions={0} | all-to-all | bytes 458752 | tf_op jit(solution)/shard_map/all_to_all | solution.py:597
  28.1 10.0 %all_to_all.11 = bf16[4,224,128]{2,1,0:T(8,128)(2,1)} all-to-all(bf16[4,224,128]{2,1,0:T(8,128)(2,1)S(1)} %broadcast_in_dim.8), channel_id=1, replica_groups=mesh['y_hi'=2,'x'=4,'z'=8,'core'=2,'y_lo'=4] {'x'}, dimensions={0} | all-to-all | bytes 458752 | tf_op jit(solution)/shard_map/all_to_all | solution.py:597
  38.1 0.0 all-gather.2.cloned.1.call-update
  38.2 34.5 %shard_map.114.taper_hbm = bf16[15,1024,1024]{2,1,0:T(8,128)(2,1)} custom-call(s32[8]{0:T(128)} %order_hbm.5, s32[8,128]{1,0:T(8,128)} %get-tuple-element.10.first_hbm, f32[4]{0:T(128)} %vert_hbm.3, f32[16]{0:T(128)} %horiz_hbm.3, s32[8,3072]{1,0:T(8,128)} %cell_hbm.3, s32[8,3072]{1,0:T(8,128)} %lev_hbm.3), custom_call_target="tpu_custom_call" | custom-call | flops 16106127360 | bytes 33554432 | tf_op jit(solution)/shard_map/pallas_call | solution.py:536
  72.6 11.7 %all-gather.2.cloned.1.call-done.got_hbm = bf16[14336,128]{1,0:T(8,128)(2,1)} async-done(((bf16[896,128]{1,0:T(8,128)(2,1)}), bf16[14336,128]{1,0:T(8,128)(2,1)}) %all-gather.2.cloned.1.call-update) | async-done | bytes 3670032 | tf_op jit(solution)/shard_map/all_gather | solution.py:624
  84.3 34.9 %shard_map.115 = (f32[80,1,512]{2,1,0:T(1,128)}, f32[1,512]{1,0:T(1,128)}) custom-call(s32[2]{0:T(128)} %pad_add_fusion.where_ref, s32[8]{0:T(128)} %order_hbm.5, s32[8,128]{1,0:T(8,128)} %get-tuple-element.10.first_hbm, f32[4]{0:T(128)} %vert_hbm.3, f32[16]{0:T(128)} %horiz_hbm.3, bf16[14336,128]{1,0:T(8,128)(2,1)} %all-gather.2.cloned.1.call-done.got_hbm, ...), custom_call_target="tpu_custom_call" | custom-call | tf_op jit(solution)/shard_map/pallas_call | solution.py:567
  (2 shorter events, 0.1 us)
Async XLA Ops:
  7.2 77.2 %all-gather.2.cloned.1.call-start = ((), (), s32[]{:S(2)}) async-start(), calls=%async_computation.2 | async-start | bytes 3899392 | tf_op jit(solution)/shard_map/all_gather | solution.py:624
Sparse Core Ops, SparseCore 0:
  38.3 46.0 all-gather.1

commit v8 on v7

--- a/solution.py
+++ b/solution.py
@@ -339,6 +339,7 @@
     prior,
     coeffs,
     lines,
+    gain,
     bufs,
     fetched,
     arrived,
@@ -434,27 +435,25 @@
         for j in range(0, NOBS, SPAN):
             part = slice(j, j + SPAN)
             cov = jnp.dot(lhs, prior[slot, :, part], preferred_element_type=F32)
-            gain = jnp.concatenate(
+            mixed = jnp.concatenate(
                 [
                     (cov[a * TY : (a + 1) * TY] * (weight_x[a : a + 1, part] * weight_y[:, part])).astype(BF16)
                     for a in range(TX)
                 ],
                 axis=0,
             )
-            change = change + jnp.dot(gain, coeffs[slot, part], preferred_element_type=F32)
+            change = change + jnp.dot(mixed, coeffs[slot, part], preferred_element_type=F32)
         return cells - change
 
     def pair_update(slot, cells, n):
         scale = lines[slot, 0:1]
         lhs = cells.astype(BF16)
         taper = bufs.at[n % 2]
-        change = jnp.zeros((TILE, WIDE), F32)
         for j in range(0, NOBS, SPAN):
             part = slice(j, j + SPAN)
             cov = jnp.dot(lhs, prior[slot, :, part], preferred_element_type=F32)
-            gain = taper[:, part] * (cov * scale[:, part]).astype(BF16)
-            change = change + jnp.dot(gain, coeffs[slot, part], preferred_element_type=F32)
-        return cells - change
+            gain[:, part] = taper[:, part] * (cov * scale[:, part]).astype(BF16)
+        return cells - jnp.dot(gain[...], coeffs[slot], preferred_element_type=F32)
 
     def next_taper(n):
         taper_copy(n).wait()
@@ -584,6 +583,7 @@
             VMEM((2, WIDE, NOBS), BF16),
             VMEM((2, NOBS, WIDE), BF16),
             VMEM((2, 8, NOBS), F32),
+            VMEM((TILE, NOBS), BF16),
             VMEM((2, TILE, NOBS), BF16),
             DMA((6,)),
             DMA((PARTS,)),

time: 127 us -> 127 us (level)
  no operation moved by 1% of the time
where the time goes in v8:
time: 127 us; the launch traced here: 126 us
  Pallas kernels  73.2 us (58%)
  blocking collectives  26.7 us (21%)
  between operations  14.1 us (11%)
  waiting for transfers between devices  11.7 us (9%)
    pallas_call x1, Pallas kernels, filter_call(): pl.pallas_call(filter_kernel, out_shape=(jax.ShapeDtypeStruct((MEMBERS, 1...  35.3 us
    pallas_call x1, Pallas kernels, taper_call(): pl.pallas_call(taper_kernel, out_shape=jax.ShapeDtypeStruct((NTILES, TILE...  34.5 us
    all_to_all x2, blocking collectives, exchange(): return lax.all_to_all(block, axes, 0, 0)  26.7 us
    all_gather x1, waiting for transfers between devices, shards(): got = lax.all_gather(group, ('z', 'core'), axis=0, tiled=True)  11.7 us
    pallas_call x1, Pallas kernels, select_call(): pl.pallas_call(select_kernel, out_shape=(jax.ShapeDtypeStruct((2 * NLEV,...  3.49 us
  transfers between devices with their start and end apart: 1, of which 1 were waited for; matrix products, arithmetic and copies ran while one was open for 0% of the time, Pallas kernels for 27%

profile of v8, /device:TPU:1, one launch (start us, length us, event | category | flops | bytes accessed | tf_op | source)
XLA Modules:
  0.0 126.5 jit_solution(7888948115016425890)
XLA Ops:
  7.2 0.0 all-gather.2.cloned.1.call-start
  7.2 0.7 pad_add_fusion.where_ref
  7.9 3.5 %shard_map.113 = (bf16[8,112,128]{2,1,0:T(8,128)(2,1)}, s32[8,128]{1,0:T(8,128)}) custom-call(s32[2]{0:T(128)} %pad_add_fusion.where_ref, s32[8]{0:T(128)} %order_hbm.5, s32[8,128]{1,0:T(8,128)} %count_hbm.1, s32[8,3072]{1,0:T(8,128)} %cell_hbm.3, s32[8,3072]{1,0:T(8,128)} %lev_hbm.3, f32[8,3072]{1,0:T(8,128)} %value_hbm.1, f32[8,3072]{1,0:T(8,128)} %var_hbm.1, ...), custom_call_target="tpu_custom_call" | custom-call | tf_op jit(solution)/shard_map/pallas_call | solution.py:510
  11.4 16.7 %all_to_all.10 = bf16[8,112,128]{2,1,0:T(8,128)(2,1)S(1)} all-to-all(bf16[8,112,128]{2,1,0:T(8,128)(2,1)} %get-tuple-element.8), channel_id=1, replica_groups=mesh['y_hi'=2,'x'=4,'z'=8,'core'=2,'y_lo'=4] {'y_hi','y_lo'}, dimensions={0} | all-to-all | bytes 458752 | tf_op jit(solution)/shard_map/all_to_all | solution.py:597
  28.1 10.0 %all_to_all.11 = bf16[4,224,128]{2,1,0:T(8,128)(2,1)} all-to-all(bf16[4,224,128]{2,1,0:T(8,128)(2,1)S(1)} %broadcast_in_dim.8), channel_id=1, replica_groups=mesh['y_hi'=2,'x'=4,'z'=8,'core'=2,'y_lo'=4] {'x'}, dimensions={0} | all-to-all | bytes 458752 | tf_op jit(solution)/shard_map/all_to_all | solution.py:597
  38.1 0.0 all-gather.2.cloned.1.call-update
  38.2 34.5 %shard_map.114.taper_hbm = bf16[15,1024,1024]{2,1,0:T(8,128)(2,1)} custom-call(s32[8]{0:T(128)} %order_hbm.5, s32[8,128]{1,0:T(8,128)} %get-tuple-element.10.first_hbm, f32[4]{0:T(128)} %vert_hbm.3, f32[16]{0:T(128)} %horiz_hbm.3, s32[8,3072]{1,0:T(8,128)} %cell_hbm.3, s32[8,3072]{1,0:T(8,128)} %lev_hbm.3), custom_call_target="tpu_custom_call" | custom-call | flops 16106127360 | bytes 33554432 | tf_op jit(solution)/shard_map/pallas_call | solution.py:535
  72.6 11.7 %all-gather.2.cloned.1.call-done.got_hbm = bf16[14336,128]{1,0:T(8,128)(2,1)} async-done(((bf16[896,128]{1,0:T(8,128)(2,1)}), bf16[14336,128]{1,0:T(8,128)(2,1)}) %all-gather.2.cloned.1.call-update) | async-done | bytes 3670032 | tf_op jit(solution)/shard_map/all_gather | solution.py:624
  84.3 35.3 %shard_map.115 = (f32[80,1,512]{2,1,0:T(1,128)}, f32[1,512]{1,0:T(1,128)}) custom-call(s32[2]{0:T(128)} %pad_add_fusion.where_ref, s32[8]{0:T(128)} %order_hbm.5, s32[8,128]{1,0:T(8,128)} %get-tuple-element.10.first_hbm, f32[4]{0:T(128)} %vert_hbm.3, f32[16]{0:T(128)} %horiz_hbm.3, bf16[14336,128]{1,0:T(8,128)(2,1)} %all-gather.2.cloned.1.call-done.got_hbm, ...), custom_call_target="tpu_custom_call" | custom-call | tf_op jit(solution)/shard_map/pallas_call | solution.py:566
  (2 shorter events, 0.1 us)
Async XLA Ops:
  7.2 77.2 %all-gather.2.cloned.1.call-start = ((), (), s32[]{:S(2)}) async-start(), calls=%async_computation.2 | async-start | bytes 3899392 | tf_op jit(solution)/shard_map/all_gather | solution.py:624
Sparse Core Ops, SparseCore 0:
  38.3 46.0 all-gather.1
